TPU v7x, 512 devices: a whole 4x8x8 slice. The times are simulated.
512 devices in a mesh: dp: 64 (over z, y), ctx: 8 (over x, core).
Axes of the slice: x: 4, y: 8, z: 8, core: 2. Of those that a mesh axis runs over, the one named last changes fastest.
Arguments:
- queries: bfloat16 [65536, 4096], P(('dp', 'ctx')), may hold values from -6 to 6
- key_rows: bfloat16 [65536, 512], P(('dp', 'ctx')), may hold values from -6 to 6
- value_rows: bfloat16 [65536, 512], P(('dp', 'ctx')), may hold values from -6 to 6
- out_grad: bfloat16 [65536, 4096], P(('dp', 'ctx')), may hold values from -6 to 6
- doc_lengths: int32 [128, 8], P('dp'), may hold values from 1 to 256, 512 in all within a row
- served_positions: int32 [64, 8, 64, 2], P('dp', 'ctx'), may hold values from 0 to 511, as said below
Outputs:
- attended: bfloat16 [65536, 4096], P(('dp', 'ctx'))
- log_sum_exp: float32 [65536, 32], P(('dp', 'ctx'))
- query_grad: bfloat16 [65536, 4096], P(('dp', 'ctx'))
Inputs may be any that keep to these rules, and one draw needn't show every extreme that they name: For each j and s, the entries served_positions[j, c, i, s * 1 + t] over all c, i and t hold every position 0 to 511 exactly once. `doc_lengths`: each row sums to 512.
All inputs are finite; a program needn't handle non-finite values.
Results may differ from a plain program's by a relative error of at most 0.033.
Values may be sent and summed in bfloat16 or wider, within the bound.
A program may use at most 128 MiB of HBM per device.

v0:
```python
import math

import jax
import jax.numpy as jnp
from jax import lax
from jax.sharding import PartitionSpec as P

HEAD_DIM = 128
HEADS = 32
KV_HEADS = 4
SUBS = 2


NEG_FILL = -1e30


def local(queries, key_rows, value_rows, out_grad, doc_lengths, served_positions):
    peer_count = lax.axis_size("dp")
    ctx_count = lax.axis_size("ctx")
    tok_rows, feature = queries.shape
    kv_width = key_rows.shape[1]
    per_peer = tok_rows // peer_count
    sub_count = SUBS
    each_sub = per_peer // sub_count
    sub_rows = peer_count * each_sub
    key_half = tok_rows // sub_count
    head_count = HEADS
    kv_heads = KV_HEADS
    head_dim = HEAD_DIM
    group_size = head_count // kv_heads
    score_scale = 1.0 / math.sqrt(head_dim)
    row_count = peer_count * per_peer

    def to_sub_major(array):
        rest = array.shape[2:]
        shaped = array.reshape((peer_count, sub_count, each_sub) + rest)
        return jnp.swapaxes(shaped, 0, 1).reshape((row_count,) + rest)

    def from_sub_major(array):
        rest = array.shape[1:]
        shaped = array.reshape((sub_count, peer_count, each_sub) + rest)
        return jnp.swapaxes(shaped, 0, 1).reshape((peer_count, per_peer) + rest)

    outgoing = (
        queries.reshape(peer_count, per_peer, feature),
        out_grad.reshape(peer_count, per_peer, feature),
    )
    recv_query, recv_grad = (
        lax.all_to_all(outgoing[0], "dp", split_axis=0, concat_axis=0, tiled=True),
        lax.all_to_all(outgoing[1], "dp", split_axis=0, concat_axis=0, tiled=True),
    )
    query_heads = to_sub_major(recv_query).reshape(row_count, head_count, head_dim)
    grad_heads = to_sub_major(recv_grad).reshape(row_count, head_count, head_dim)
    query_pos = to_sub_major(served_positions.reshape(peer_count, per_peer))
    query_sub = jnp.arange(row_count, dtype=jnp.int32) // sub_rows
    doc_ends = jnp.cumsum(doc_lengths, axis=1)
    sub_ids = jnp.arange(sub_count, dtype=jnp.int32)
    counts = jnp.sum((query_pos[:, None, None] >= doc_ends[None]).astype(jnp.int32), axis=2)
    query_doc = jnp.sum(jnp.where(query_sub[:, None] == sub_ids[None, :], counts, 0), axis=1)

    def group_product(source_heads, key_piece, head_idx):
        source_group = source_heads[:, head_idx * group_size : (head_idx + 1) * group_size, :]
        key_head = key_piece[:, head_idx * head_dim : (head_idx + 1) * head_dim]
        return jnp.einsum("nhd,kd->hnk", source_group, key_head, preferred_element_type=jnp.float32)

    key_all, value_all = (
        lax.all_gather(key_rows, "ctx", axis=0, tiled=True),
        lax.all_gather(value_rows, "ctx", axis=0, tiled=True),
    )
    key_split = key_all.reshape(ctx_count, sub_count, key_half, kv_width)
    value_split = value_all.reshape(ctx_count, sub_count, key_half, kv_width)
    seq_len = ctx_count * key_half
    key_pos = jnp.arange(seq_len, dtype=jnp.int32)
    out_subs, lse_subs, dq_subs = ([], [], [])
    for sub_idx in range(sub_count):
        keys_sub = key_split[:, sub_idx].reshape(seq_len, kv_width)
        values_sub = value_split[:, sub_idx].reshape(seq_len, kv_width)
        lower = sub_idx * sub_rows
        rows_query = query_heads[lower : lower + sub_rows]
        rows_grad = grad_heads[lower : lower + sub_rows]
        rows_pos = query_pos[lower : lower + sub_rows]
        rows_doc = query_doc[lower : lower + sub_rows]
        key_doc = jnp.sum(
            (key_pos[:, None] >= doc_ends[sub_idx][None, :]).astype(jnp.int32), axis=1
        )
        visible = (key_pos[None, :] <= rows_pos[:, None]) & (key_doc[None, :] == rows_doc[:, None])
        out_list, lse_list, dq_list = ([], [], [])
        for head_idx in range(kv_heads):
            masked = jnp.where(
                visible[None], score_scale * group_product(rows_query, keys_sub, head_idx), NEG_FILL
            )
            group_max = jnp.max(masked, axis=-1)
            group_sum = jnp.sum(
                jnp.where(visible[None], jnp.exp(masked - group_max[..., None]), 0.0), axis=-1
            )
            group_lse = group_max + jnp.log(group_sum)
            weights = jnp.where(visible[None], jnp.exp(masked - group_lse[..., None]), 0.0)
            value_head = values_sub[:, head_idx * head_dim : (head_idx + 1) * head_dim]
            key_head = keys_sub[:, head_idx * head_dim : (head_idx + 1) * head_dim]
            out_group = jnp.einsum(
                "hnk,kd->nhd",
                weights.astype(jnp.bfloat16),
                value_head,
                preferred_element_type=jnp.float32,
            ).astype(jnp.bfloat16)
            grad_group = rows_grad[:, head_idx * group_size : (head_idx + 1) * group_size, :]
            delta_group = jnp.einsum(
                "nhd,nhd->hn", grad_group, out_group, preferred_element_type=jnp.float32
            )
            prob_grad = group_product(rows_grad, values_sub, head_idx)
            score_grad = (weights * (prob_grad - delta_group[..., None])).astype(jnp.bfloat16)
            dq_list.append(
                jnp.einsum("hnk,kd->nhd", score_grad, key_head, preferred_element_type=jnp.float32)
            )
            out_list.append(out_group)
            lse_list.append(group_lse)
        out_subs.append(jnp.concatenate(out_list, axis=1))
        lse_subs.append(jnp.stack(lse_list))
        dq_subs.append(jnp.concatenate(dq_list, axis=1))
    attended = jnp.concatenate(out_subs, axis=0)
    lse_heads = jnp.concatenate(lse_subs, axis=2)
    grad_sum = jnp.concatenate(dq_subs, axis=0)
    lse_rows = from_sub_major(lse_heads.reshape(head_count, row_count).T)
    lse_home = lax.all_to_all(lse_rows, "dp", split_axis=0, concat_axis=0, tiled=True)
    out_send = from_sub_major(attended.reshape(row_count, feature))
    grad_send = from_sub_major(
        (score_scale * grad_sum).astype(jnp.bfloat16).reshape(row_count, feature)
    )
    out_home, grad_home = (
        lax.all_to_all(out_send, "dp", split_axis=0, concat_axis=0, tiled=True),
        lax.all_to_all(grad_send, "dp", split_axis=0, concat_axis=0, tiled=True),
    )
    return (
        out_home.reshape(tok_rows, feature),
        lse_home.reshape(tok_rows, head_count),
        grad_home.reshape(tok_rows, feature),
    )


def solution(mesh):
    in_specs = (
        P(("dp", "ctx"), None),
        P(("dp", "ctx"), None),
        P(("dp", "ctx"), None),
        P(("dp", "ctx"), None),
        P("dp", None),
        P("dp", "ctx", None, None),
    )
    out_specs = (P(("dp", "ctx"), None), P(("dp", "ctx"), None), P(("dp", "ctx"), None))
    return jax.shard_map(local, mesh=mesh, in_specs=in_specs, out_specs=out_specs, check_vma=False)
```

profile of v0, /device:TPU:1, one launch (start us, length us, event | category | flops | bytes accessed | tf_op | source)
XLA Modules:
  0.0 257.2 jit_solution(2035588538977584752)
XLA Ops:
  7.2 0.7 all-gather.3.cloned.1.call-update
  7.9 2.5 reshape.379
  10.4 17.3 %all-to-all-start = ((bf16[64,2,4096]{2,1,0:T(2,128)(2,1)}), bf16[64,2,4096]{2,1,0:T(2,128)(2,1)S(1)}, u32[]{:S(2)}, u32[]{:S(2)}) async-start(bf16[64,2,4096]{2,1,0:T(2,128)(2,1)} %reshape.379), calls=%async_computation | async-start | bytes 2097152 | tf_op jit(solution)/shard_map/all_to_all | solution.py:49
  27.8 0.7 all-gather.5.cloned.1.call-update
  28.6 1.5 reshape.388
  30.7 14.1 %all-gather.3.cloned.1.call-done = bf16[1024,512]{1,0:T(8,128)(2,1)} async-done(((bf16[128,512]{1,0:T(8,128)(2,1)}), bf16[1024,512]{1,0:T(8,128)(2,1)}) %all-gather.3.cloned.1.call-update) | async-done | bytes 1048592 | tf_op jit(solution)/shard_map/all_gather | solution.py:67
  44.8 2.3 fusion.181
  47.1 28.7 %all-gather.5.cloned.1.call-done = bf16[1024,512]{1,0:T(8,128)(2,1)} async-done(((bf16[128,512]{1,0:T(8,128)(2,1)}), bf16[1024,512]{1,0:T(8,128)(2,1)}) %all-gather.5.cloned.1.call-update) | async-done | bytes 1048592 | tf_op jit(solution)/shard_map/all_gather | solution.py:68
  75.7 2.3 fusion.180
  78.0 12.8 %all-to-all-start.3 = ((bf16[64,2,4096]{2,1,0:T(2,128)(2,1)}), bf16[64,2,4096]{2,1,0:T(2,128)(2,1)S(1)}, u32[]{:S(2)}, u32[]{:S(2)}) async-start(bf16[64,2,4096]{2,1,0:T(2,128)(2,1)} %reshape.388), calls=%async_computation.3 | async-start | bytes 2097152 | tf_op jit(solution)/shard_map/all_to_all | solution.py:50
  90.9 6.2 %slice_reduce_fusion.3 = (bf16[64,4096]{1,0:T(8,128)(2,1)S(1)}, bf16[64,4096]{1,0:T(8,128)(2,1)}) fusion(bf16[2,64,1,4096]{3,0,1,2:T(2,128)(2,1)S(1)} %bitcast.353), kind=kLoop, calls=%fused_computation.85 | loop fusion | bytes 2097152 | tf_op jit(solution)/shard_map/slice | solution.py:79
  97.3 0.8 copy-done.9
  99.9 1.3 select_reduce_fusion.7
  101.3 17.7 %all-to-all-done.3 = bf16[64,2,4096]{2,1,0:T(2,128)(2,1)S(1)} async-done(((bf16[64,2,4096]{2,1,0:T(2,128)(2,1)}), bf16[64,2,4096]{2,1,0:T(2,128)(2,1)S(1)}, u32[]{:S(2)}, u32[]{:S(2)}) %all-to-all-start.3) | async-done | bytes 1048608 | tf_op jit(solution)/shard_map/all_to_all | solution.py:50
  119.0 6.4 %slice_reduce_fusion.1 = (bf16[64,4096]{1,0:T(8,128)(2,1)S(1)}, bf16[64,4096]{1,0:T(8,128)(2,1)}) fusion(bf16[2,64,1,4096]{3,0,1,2:T(2,128)(2,1)S(1)} %bitcast.354), kind=kLoop, calls=%fused_computation.83 | loop fusion | bytes 2097152 | tf_op jit(solution)/shard_map/slice | solution.py:80
  125.5 0.8 fusion.182
  126.7 1.9 fusion.136
  128.6 2.0 fusion.56
  130.6 2.0 fusion.135
  132.6 2.3 fusion.55
  134.9 2.1 fusion.134
  137.0 2.2 fusion.54
  139.1 2.0 fusion.133
  141.1 1.3 fusion.53
  142.6 0.8 copy-done.7
  145.0 1.3 select_reduce_fusion.3
  146.4 0.8 fusion.183
  147.2 1.9 fusion.132
  149.2 2.6 %fusion.52 = f32[64,8,128]{2,0,1:T(8,128)} fusion(f32[8,64,512]{2,1,0:T(8,128)} %copy-done.4, f32[8,64]{1,0:T(8,128)S(1)} %get-tuple-element.78, f32[8,64]{1,0:T(8,128)S(1)} %log_add_fusion.3, pred[64,512]{1,0:T(8,128)(4,1)S(1)} %fusion.146, bf16[64,8,128]{2,1,0:T(8,128)(2,1)} %copy-done.27, bf16[512,512]{1,0:T(8,128)(2,1)} %bitcast.365, ...), kind=kOutput, calls=%fused_computation.69 | convolution fusion | flops 135528448 | bytes 1740800 | tf_op jit(solution)/shard_map/hnk,kd->nhd/dot_general | solution.py:113
  151.8 2.0 fusion.131
  153.8 2.3 fusion.51
  156.1 2.1 fusion.130
  158.1 2.2 fusion.50
  160.3 1.9 fusion.129
  162.2 2.2 fusion.49
  164.6 0.7 copy.126
  165.3 7.6 %all-to-all-start.2 = ((f32[64,2,32]{2,1,0:T(2,128)}), f32[64,2,32]{2,1,0:T(2,128)S(1)}, u32[]{:S(2)}, u32[]{:S(2)}) async-start(f32[64,2,32]{2,1,0:T(2,128)} %copy.126), calls=%async_computation.2 | async-start | bytes 131072 | tf_op jit(solution)/shard_map/all_to_all | solution.py:124
  173.0 1.4 fusion
  174.4 0.7 copy.135
  175.6 2.1 copy.136
  177.7 6.1 %all-to-all-done.2 = f32[64,2,32]{2,1,0:T(2,128)S(1)} async-done(((f32[64,2,32]{2,1,0:T(2,128)}), f32[64,2,32]{2,1,0:T(2,128)S(1)}, u32[]{:S(2)}, u32[]{:S(2)}) %all-to-all-start.2) | async-done | bytes 16416 | tf_op jit(solution)/shard_map/all_to_all | solution.py:124
  183.9 6.0 %all-to-all-start.4 = ((bf16[64,2,4096]{2,1,0:T(2,128)(2,1)}), bf16[64,2,4096]{2,1,0:T(2,128)(2,1)S(1)}, u32[]{:S(2)}, u32[]{:S(2)}) async-start(bf16[64,2,4096]{2,1,0:T(2,128)(2,1)} %copy.136), calls=%async_computation.4 | async-start | bytes 2097152 | tf_op jit(solution)/shard_map/all_to_all | solution.py:131
  191.2 2.1 copy.125
  193.2 22.4 %all-to-all-done.4 = bf16[64,2,4096]{2,1,0:T(2,128)(2,1)S(1)} async-done(((bf16[64,2,4096]{2,1,0:T(2,128)(2,1)}), bf16[64,2,4096]{2,1,0:T(2,128)(2,1)S(1)}, u32[]{:S(2)}, u32[]{:S(2)}) %all-to-all-start.4) | async-done | bytes 1048608 | tf_op jit(solution)/shard_map/all_to_all | solution.py:131
  215.6 8.2 %all-to-all-start.1 = ((bf16[64,2,4096]{2,1,0:T(2,128)(2,1)}), bf16[64,2,4096]{2,1,0:T(2,128)(2,1)S(1)}, u32[]{:S(2)}, u32[]{:S(2)}) async-start(bf16[64,2,4096]{2,1,0:T(2,128)(2,1)} %copy.125), calls=%async_computation.1 | async-start | bytes 2097152 | tf_op jit(solution)/shard_map/all_to_all | solution.py:130
  224.6 1.2 reshape.391
  225.7 23.4 %all-to-all-done.1 = bf16[64,2,4096]{2,1,0:T(2,128)(2,1)S(1)} async-done(((bf16[64,2,4096]{2,1,0:T(2,128)(2,1)}), bf16[64,2,4096]{2,1,0:T(2,128)(2,1)S(1)}, u32[]{:S(2)}, u32[]{:S(2)}) %all-to-all-start.1) | async-done | bytes 1048608 | tf_op jit(solution)/shard_map/all_to_all | solution.py:130
  249.2 1.2 reshape.383
  (103 shorter events, 7.8 us)
Async XLA Ops:
  7.2 37.6 %all-gather.3.cloned.1.call-start = ((), (), s32[]{:S(2)}) async-start(), calls=%async_computation.5 | async-start | bytes 1179648 | tf_op jit(solution)/shard_map/all_gather | solution.py:67
  10.4 18.0 %copy-start.30 = (s32[1,1,64,2]{2,3,1,0:T(2,128)S(1)}, s32[1,1,64,2]{2,3,1,0:T(2,128)}, u32[]{:S(2)}) copy-start(s32[1,1,64,2]{2,3,1,0:T(2,128)} %param.11) | copy-start | bytes 1540
  10.4 18.1 %copy-start.11 = (bf16[128,4096]{1,0:T(8,128)(2,1)S(1)}, bf16[128,4096]{1,0:T(8,128)(2,1)}, u32[]{:S(2)}) copy-start(bf16[128,4096]{1,0:T(8,128)(2,1)} %param.9) | copy-start | bytes 3145732
  10.4 67.6 %all-to-all-start = ((bf16[64,2,4096]{2,1,0:T(2,128)(2,1)}), bf16[64,2,4096]{2,1,0:T(2,128)(2,1)S(1)}, u32[]{:S(2)}, u32[]{:S(2)}) async-start(bf16[64,2,4096]{2,1,0:T(2,128)(2,1)} %reshape.379), calls=%async_computation | async-start | bytes 2097152 | tf_op jit(solution)/shard_map/all_to_all | solution.py:49
  27.7 48.0 %all-gather.5.cloned.1.call-start = ((), (), s32[]{:S(2)}) async-start(), calls=%async_computation.6 | async-start | bytes 1179648 | tf_op jit(solution)/shard_map/all_gather | solution.py:68
  28.6 1.5 copy-start.29
  78.0 40.9 %all-to-all-start.3 = ((bf16[64,2,4096]{2,1,0:T(2,128)(2,1)}), bf16[64,2,4096]{2,1,0:T(2,128)(2,1)S(1)}, u32[]{:S(2)}, u32[]{:S(2)}) async-start(bf16[64,2,4096]{2,1,0:T(2,128)(2,1)} %reshape.388), calls=%async_computation.3 | async-start | bytes 2097152 | tf_op jit(solution)/shard_map/all_to_all | solution.py:50
  97.1 1.0 copy-start.9
  98.9 1.0 copy-start.2
  99.3 2.0 copy-start
  125.4 1.4 copy-start.3
  126.2 2.4 copy-start.28
  128.6 2.0 copy-start.1
  134.9 2.1 copy-start.10
  134.9 2.1 copy-start.13
  139.1 2.0 copy-start.26
  141.1 1.3 copy-start.5
  142.4 1.0 copy-start.7
  144.2 3.0 %copy-start.4 = (f32[8,64,512]{2,1,0:T(8,128)}, f32[8,64,512]{2,1,0:T(8,128)S(1)}, u32[]{:S(2)}) copy-start(f32[8,64,512]{2,1,0:T(8,128)S(1)} %get-tuple-element.59) | copy-start | bytes 3145732
  145.0 1.3 copy-start.6
  147.2 1.9 copy-start.27
  156.1 2.1 copy-start.8
  156.1 2.1 copy-start.12
  162.2 10.8 %copy-start.14 = (f32[64,8,128]{2,0,1:T(8,128)S(1)}, f32[64,8,128]{2,0,1:T(8,128)}, u32[]{:S(2)}) copy-start(f32[64,8,128]{2,0,1:T(8,128)} %fusion.55) | copy-start | bytes 786436
  162.2 10.8 %copy-start.15 = (f32[64,8,128]{2,0,1:T(8,128)S(1)}, f32[64,8,128]{2,0,1:T(8,128)}, u32[]{:S(2)}) copy-start(f32[64,8,128]{2,0,1:T(8,128)} %fusion.54) | copy-start | bytes 786436
  162.2 10.8 %copy-start.16 = (f32[64,8,128]{2,0,1:T(8,128)S(1)}, f32[64,8,128]{2,0,1:T(8,128)}, u32[]{:S(2)}) copy-start(f32[64,8,128]{2,0,1:T(8,128)} %fusion.53) | copy-start | bytes 786436
  162.2 10.8 %copy-start.17 = (f32[64,8,128]{2,0,1:T(8,128)S(1)}, f32[64,8,128]{2,0,1:T(8,128)}, u32[]{:S(2)}) copy-start(f32[64,8,128]{2,0,1:T(8,128)} %fusion.52) | copy-start | bytes 786436
  165.3 18.5 %all-to-all-start.2 = ((f32[64,2,32]{2,1,0:T(2,128)}), f32[64,2,32]{2,1,0:T(2,128)S(1)}, u32[]{:S(2)}, u32[]{:S(2)}) async-start(f32[64,2,32]{2,1,0:T(2,128)} %copy.126), calls=%async_computation.2 | async-start | bytes 131072 | tf_op jit(solution)/shard_map/all_to_all | solution.py:124
  177.7 12.1 %copy-start.18 = (bf16[8,64,128]{2,1,0:T(8,128)(2,1)S(1)}, bf16[8,64,128]{2,1,0:T(8,128)(2,1)}, u32[]{:S(2)}) copy-start(bf16[8,64,128]{2,1,0:T(8,128)(2,1)} %get-tuple-element.87) | copy-start | bytes 393220
  177.7 12.1 %copy-start.19 = (bf16[8,64,128]{2,1,0:T(8,128)(2,1)S(1)}, bf16[8,64,128]{2,1,0:T(8,128)(2,1)}, u32[]{:S(2)}) copy-start(bf16[8,64,128]{2,1,0:T(8,128)(2,1)} %get-tuple-element.85) | copy-start | bytes 393220
  177.7 12.2 %copy-start.20 = (bf16[8,64,128]{2,1,0:T(8,128)(2,1)S(1)}, bf16[8,64,128]{2,1,0:T(8,128)(2,1)}, u32[]{:S(2)}) copy-start(bf16[8,64,128]{2,1,0:T(8,128)(2,1)} %get-tuple-element.83) | copy-start | bytes 393220
  177.7 12.2 %copy-start.21 = (bf16[8,64,128]{2,1,0:T(8,128)(2,1)S(1)}, bf16[8,64,128]{2,1,0:T(8,128)(2,1)}, u32[]{:S(2)}) copy-start(bf16[8,64,128]{2,1,0:T(8,128)(2,1)} %get-tuple-element.81) | copy-start | bytes 393220
  177.7 12.2 %copy-start.22 = (bf16[8,64,128]{2,1,0:T(8,128)(2,1)S(1)}, bf16[8,64,128]{2,1,0:T(8,128)(2,1)}, u32[]{:S(2)}) copy-start(bf16[8,64,128]{2,1,0:T(8,128)(2,1)} %get-tuple-element.79) | copy-start | bytes 393220
  177.7 12.2 %copy-start.23 = (bf16[8,64,128]{2,1,0:T(8,128)(2,1)S(1)}, bf16[8,64,128]{2,1,0:T(8,128)(2,1)}, u32[]{:S(2)}) copy-start(bf16[8,64,128]{2,1,0:T(8,128)(2,1)} %get-tuple-element.77) | copy-start | bytes 393220
  177.7 12.2 %copy-start.24 = (bf16[8,64,128]{2,1,0:T(8,128)(2,1)S(1)}, bf16[8,64,128]{2,1,0:T(8,128)(2,1)}, u32[]{:S(2)}) copy-start(bf16[8,64,128]{2,1,0:T(8,128)(2,1)} %get-tuple-element.75) | copy-start | bytes 393220
  177.7 12.2 %copy-start.25 = (bf16[8,64,128]{2,1,0:T(8,128)(2,1)S(1)}, bf16[8,64,128]{2,1,0:T(8,128)(2,1)}, u32[]{:S(2)}) copy-start(bf16[8,64,128]{2,1,0:T(8,128)(2,1)} %get-tuple-element.73) | copy-start | bytes 393220
  183.9 31.8 %all-to-all-start.4 = ((bf16[64,2,4096]{2,1,0:T(2,128)(2,1)}), bf16[64,2,4096]{2,1,0:T(2,128)(2,1)S(1)}, u32[]{:S(2)}, u32[]{:S(2)}) async-start(bf16[64,2,4096]{2,1,0:T(2,128)(2,1)} %copy.136), calls=%async_computation.4 | async-start | bytes 2097152 | tf_op jit(solution)/shard_map/all_to_all | solution.py:131
  215.6 33.5 %all-to-all-start.1 = ((bf16[64,2,4096]{2,1,0:T(2,128)(2,1)}), bf16[64,2,4096]{2,1,0:T(2,128)(2,1)S(1)}, u32[]{:S(2)}, u32[]{:S(2)}) async-start(bf16[64,2,4096]{2,1,0:T(2,128)(2,1)} %copy.125), calls=%async_computation.1 | async-start | bytes 2097152 | tf_op jit(solution)/shard_map/all_to_all | solution.py:130
Sparse Core Ops, SparseCore 0:
  10.1 34.5 all-gather.2
  46.9 28.7 all-gather.4
where the time goes:
time: 262 us; the launch traced here: 257 us
  waiting for transfers between devices  114 us (44%)
  starting transfers between devices  52 us (20%)
  local copies, waits for them, and re-layouts  36.3 us (14%)
  matrix products  35.8 us (14%)
  between operations  14.5 us (6%)
  other arithmetic  4.81 us (2%)
    all_gather x1, waiting for transfers between devices, local(): lax.all_gather(value_rows, 'ctx', axis=0, tiled=True)  28.7 us
    all_to_all x1, waiting for transfers between devices, local(): lax.all_to_all(out_send, 'dp', split_axis=0, concat_axis=0, tiled=True)  23.4 us
    all_to_all x1, waiting for transfers between devices, local(): lax.all_to_all(grad_send, 'dp', split_axis=0, concat_axis=0, tiled=True)  22.4 us
    all_to_all x1, waiting for transfers between devices, local(): lax.all_to_all(outgoing[1], 'dp', split_axis=0, concat_axis=0, tiled=True)  17.7 us
    all_to_all x1, starting transfers between devices, local(): lax.all_to_all(outgoing[0], 'dp', split_axis=0, concat_axis=0, tiled=True)  17.3 us
    dot_general x8, matrix products, local(): jnp.einsum('hnk,kd->nhd', score_grad, key_head, preferred_element_type=jn...  17 us
    dot_general x8, matrix products, local(): jnp.einsum('hnk,kd->nhd', weights.astype(jnp.bfloat16), value_head, prefe...  15.9 us
    all_gather x1, waiting for transfers between devices, local(): lax.all_gather(key_rows, 'ctx', axis=0, tiled=True)  14.1 us
  transfers between devices with their start and end apart: 7, of which 6 were waited for; matrix products, arithmetic and copies ran while one was open for 11% of the time, Pallas kernels for 0%

commit v1 on v0

v1 whole, which is shorter than its diff:
```python
import functools
import math

import jax
import jax.numpy as jnp
from jax import lax
from jax.experimental import pallas as pl
from jax.experimental.pallas import tpu as pltpu
from jax.sharding import PartitionSpec as P

HEAD_DIM = 128
HEADS = 32
KV_HEADS = 4
GROUP = HEADS // KV_HEADS
SUBS = 2
NZ = 8
NY = 8
NX = 4
NCTX = 8
SLOTS = 32
HALF = 64
SEQ = 512
KV_ROWS = 272
NEG_FILL = -1e30
MESH = pl.DeviceIdType.MESH


def z_step(e, core):
    return e - 1 - 4 * core * (e // 3)


def kernel(rows, keys, values, info, out, lse_out, kv, got, res, lse,
           row_send, row_recv, kva_send, kvb_send, kv_recv, ring_send, ring_recv,
           res_send, res_recv, lse_send, lse_recv):
    dp = lax.axis_index("dp")
    ctx = lax.axis_index("ctx")
    z, y = dp // NY, dp % NY
    x, core = ctx // 2, ctx % 2
    right = z * NY + (y + 1) % NY
    left = z * NY + (y + NY - 1) % NY

    barrier = pltpu.get_barrier_semaphore()

    def greet(n, carry):
        other_z, other_ctx = n // NCTX, n % NCTX

        @pl.when(jnp.logical_or(other_z != z, other_ctx != ctx))
        def _():
            pl.semaphore_signal(barrier, inc=1, device_id=(other_z * NY + y, other_ctx),
                                device_id_type=MESH)

        return carry

    lax.fori_loop(0, NZ * NCTX, greet, 0)
    pl.semaphore_signal(barrier, inc=1, device_id=(left, ctx), device_id_type=MESH)
    pl.semaphore_signal(barrier, inc=1, device_id=(right, ctx), device_id_type=MESH)
    pl.semaphore_wait(barrier, NZ * NCTX + 1)

    def remote(src, dst, send, recv, dev):
        return pltpu.make_async_remote_copy(src_ref=src, dst_ref=dst, send_sem=send, recv_sem=recv,
                                            device_id=dev, device_id_type=MESH)

    def kv_parts(head, copy):
        cols = pl.ds(head * HEAD_DIM, HEAD_DIM)
        return ((keys.at[:, cols], kv.at[y, ctx, pl.ds(0, 128)]),
                (values.at[:, cols], kv.at[y, ctx, pl.ds(128, 128)]),
                (info.at[copy], kv.at[y, ctx, pl.ds(256, 16)]))

    far = ((z + 4) % NZ) * NY + y
    for head in range(KV_HEADS):
        is_self = jnp.logical_and(core == 0, x == head)

        @pl.when(is_self)
        def _(head=head):
            for src, dst in kv_parts(head, 0):
                pltpu.make_async_copy(src, dst, kv_recv).start()

        @pl.when(jnp.logical_not(is_self))
        def _(head=head):
            for src, dst in kv_parts(head, 0):
                remote(src, dst, kva_send, kv_recv, (dp, head * 2)).start()

        for src, dst in kv_parts(head, 1):
            remote(src, dst, kvb_send, kv_recv, (far, head * 2 + 1)).start()

    def send_rows(n, carry):
        copy, e, head = n % 2, (n // 2) % 4, n // 8
        server_z = (z - z_step(e, core) + 2 * NZ) % NZ
        home = (server_z + 4 * copy) % NZ
        src = rows.at[head * NZ + home]
        dst = got.at[(e % 2) * 16 + ctx * 2 + e // 2]
        is_self = jnp.logical_and(server_z == z, head * 2 + copy == ctx)

        @pl.when(is_self)
        def _():
            pltpu.make_async_copy(src, dst, row_recv).start()

        @pl.when(jnp.logical_not(is_self))
        def _():
            remote(src, dst, row_send, row_recv, (server_z * NY + y, head * 2 + copy)).start()

        return carry

    lax.fori_loop(0, SLOTS, send_rows, 0)

    def wait_bytes(ref, sem):
        pltpu.make_async_copy(ref, ref, sem).wait()

    def ring(step):
        from_left = kv.at[(y - step + NY) % NY]
        from_right = kv.at[(y + step) % NY]
        if step == 3:
            from_left = from_left.at[pl.ds(0, 4)]
            from_right = from_right.at[pl.ds(4, 4)]
        return (remote(from_left, from_left, ring_send.at[0, step], ring_recv.at[0, step], (right, ctx)),
                remote(from_right, from_right, ring_send.at[1, step], ring_recv.at[1, step], (left, ctx)))

    def ring_arrived(step):
        from_left = kv.at[(y - step - 1 + NY) % NY]
        from_right = kv.at[(y + step + 1) % NY]
        if step == 3:
            from_left = from_left.at[pl.ds(0, 4)]
            from_right = from_right.at[pl.ds(4, 4)]
        wait_bytes(from_left, ring_recv.at[0, step])
        wait_bytes(from_right, ring_recv.at[1, step])

    wait_bytes(kv.at[y], kv_recv)
    for copy in ring(0):
        copy.start()
    ring_arrived(0)
    for copy in ring(1):
        copy.start()
    ring_arrived(1)
    for copy in ring(2):
        copy.start()
    wait_bytes(got, row_recv)

    scale = 1.0 / math.sqrt(HEAD_DIM)
    to_log2 = scale * math.log2(math.e)
    lane = lax.broadcasted_iota(jnp.int32, (128, 128), 0)
    key_pos = lax.broadcasted_iota(jnp.int32, (256, SEQ), 1).astype(jnp.float32)
    lse_lane = lax.broadcasted_iota(jnp.int32, (256, 128), 1)
    server_home = (z + 4 * core) % NZ

    def pick(base):
        return jnp.where(lane == base, 16.0, jnp.where(lane == base + 1, 1.0, 0.0)).astype(jnp.bfloat16)

    def dot(a, b, dims):
        return lax.dot_general(a, b, (dims, ((), ())), preferred_element_type=jnp.float32)

    def one_sequence(y0, s):
        t = y0 * SUBS + s
        q = got[:, 0, t].reshape(256, HEAD_DIM)
        g = got[:, 1, t].reshape(256, HEAD_DIM)
        k = kv[y0, :, pl.ds(pl.multiple_of(s * HALF, HALF), HALF), :].reshape(SEQ, HEAD_DIM)
        v = kv[y0, :, pl.ds(pl.multiple_of(128 + s * HALF, HALF), HALF), :].reshape(SEQ, HEAD_DIM)
        marks = kv[y0, :, pl.ds(256, 16), :].reshape(128, 128)
        bounds = []
        for which in range(2):
            halves = [dot(marks, pick(e_lo * 64 + s * 32 + y * 4 + which * 2), ((1,), (0,)))
                      for e_lo in range(2)]
            whole = jnp.concatenate(halves, axis=0)
            bounds.append(jnp.concatenate([whole] * 4, axis=1))
        visible = jnp.logical_and(key_pos <= bounds[0], key_pos >= bounds[1])
        scores = jnp.where(visible, dot(q, k, ((1,), (1,))) * to_log2, NEG_FILL)
        top = jnp.max(scores, axis=1, keepdims=True)
        p = jnp.exp2(scores - top)
        total = jnp.sum(p, axis=1, keepdims=True)
        inverse = 1.0 / total
        att = (dot(p.astype(jnp.bfloat16), v, ((1,), (0,))) * inverse).astype(jnp.bfloat16)
        delta = jnp.sum(g.astype(jnp.float32) * att.astype(jnp.float32), axis=1, keepdims=True)
        grad = dot(g, v, ((1,), (1,)))
        ds = (p * (grad - delta)).astype(jnp.bfloat16)
        dq = (dot(ds, k, ((1,), (0,))) * (inverse * scale)).astype(jnp.bfloat16)
        res[:, y0, 0, s] = att.reshape(SLOTS, GROUP, HEAD_DIM)
        res[:, y0, 1, s] = dq.reshape(SLOTS, GROUP, HEAD_DIM)
        line = (top + jnp.log2(total)) * math.log(2.0)
        lse[...] = jnp.where(lse_lane == t, line, lse[...].reshape(256, 128)).reshape(SLOTS, GROUP, 128)

    def home_of(slot):
        e, c = (slot % 2) * 2 + slot // 16, (slot // 2) % NCTX
        home_z = (z + z_step(e, c % 2) + NZ) % NZ
        is_self = jnp.logical_and(home_z == z, c == ctx)
        return is_self, (home_z * NY + y, c)

    def serve(n, carry):
        y0 = (y + ((n + 1) // 2) * (2 * (n % 2) - 1) + NY) % NY

        def sub(s, inner):
            one_sequence(y0, s)
            return inner

        lax.fori_loop(0, SUBS, sub, 0)

        def give(slot, inner):
            is_self, dev = home_of(slot)
            src = res.at[slot, y0]
            dst = out.at[x, server_home, y0]

            @pl.when(is_self)
            def _():
                pltpu.make_async_copy(src, dst, res_recv).start()

            @pl.when(jnp.logical_not(is_self))
            def _():
                remote(src, dst, res_send, res_recv, dev).start()

            return inner

        lax.fori_loop(0, SLOTS, give, 0)
        return carry

    lse[...] = jnp.zeros_like(lse)
    lax.fori_loop(0, 3, serve, 0)
    ring_arrived(2)
    for copy in ring(3):
        copy.start()
    lax.fori_loop(3, 7, serve, 0)
    ring_arrived(3)
    lax.fori_loop(7, 8, serve, 0)

    def give_lse(slot, carry):
        is_self, dev = home_of(slot)
        src = lse.at[slot]
        dst = lse_out.at[x, server_home]

        @pl.when(is_self)
        def _():
            pltpu.make_async_copy(src, dst, lse_recv).start()

        @pl.when(jnp.logical_not(is_self))
        def _():
            remote(src, dst, lse_send, lse_recv, dev).start()

        return carry

    lax.fori_loop(0, SLOTS, give_lse, 0)

    wait_bytes(rows.at[pl.ds(0, SLOTS - 1)], row_send)
    wait_bytes(kv.at[0, pl.ds(0, 4)], kvb_send)

    @pl.when(core == 0)
    def _():
        wait_bytes(kv.at[0, pl.ds(0, 3)], kva_send)

    @pl.when(core != 0)
    def _():
        wait_bytes(kv.at[0, pl.ds(0, 4)], kva_send)

    for step in range(4):
        for copy in ring(step):
            copy.wait_send()
    wait_bytes(res.at[pl.ds(0, SLOTS - 1)], res_send)
    wait_bytes(lse.at[pl.ds(0, SLOTS - 1)], lse_send)
    wait_bytes(out, res_recv)
    wait_bytes(lse_out, lse_recv)


def local(queries, key_rows, value_rows, out_grad, doc_lengths, served_positions):
    dp = lax.axis_index("dp")
    core = lax.axis_index("ctx") % 2
    z = dp // NY

    def by_home(array):
        return array.reshape(NZ, 16, KV_HEADS, GROUP, HEAD_DIM).transpose(2, 0, 1, 3, 4)

    rows = jnp.stack([by_home(queries), by_home(out_grad)], axis=2)
    rows = rows.reshape(SLOTS, 2, 16, GROUP, HEAD_DIM)

    ends = jnp.cumsum(doc_lengths, axis=1)
    pos = served_positions.reshape(NZ, NY, SUBS)
    first = jnp.max(jnp.where(ends[None, None] <= pos[..., None], ends[None, None], 0), axis=-1)
    parts = jnp.stack([pos // 16, pos % 16, first // 16, first % 16], axis=-1)
    parts = parts.transpose(0, 2, 1, 3).reshape(NZ, HALF).astype(jnp.float32)
    slot = jnp.arange(8, dtype=jnp.int32)
    e = slot % 4
    home_z = (z + 4 * (slot // 4) + z_step(e, core) + NZ) % NZ
    chosen = home_z[:, None] == jnp.arange(NZ, dtype=jnp.int32)[None, :]
    marks = jnp.sum(jnp.where(chosen[:, :, None], parts[None], 0.0), axis=1)
    marks = marks.reshape(2, 2, 1, 128)
    info = jnp.broadcast_to(marks, (2, 2, GROUP, 128)).reshape(2, 16, 128).astype(jnp.bfloat16)

    bf16 = jnp.bfloat16
    dma = pltpu.SemaphoreType.DMA
    out, lse = pl.pallas_call(
        kernel,
        out_shape=(
            jax.ShapeDtypeStruct((KV_HEADS, NZ, NY, 2, SUBS, GROUP, HEAD_DIM), bf16),
            jax.ShapeDtypeStruct((KV_HEADS, NZ, GROUP, 128), jnp.float32),
        ),
        in_specs=[pl.BlockSpec(memory_space=pl.ANY)] * 4,
        out_specs=(pl.BlockSpec(memory_space=pl.ANY),) * 2,
        scratch_shapes=[
            pltpu.VMEM((NY, NCTX, KV_ROWS, HEAD_DIM), bf16),
            pltpu.VMEM((SLOTS, 2, 16, GROUP, HEAD_DIM), bf16),
            pltpu.VMEM((SLOTS, NY, 2, SUBS, GROUP, HEAD_DIM), bf16),
            pltpu.VMEM((SLOTS, GROUP, 128), jnp.float32),
            dma, dma, dma, dma, dma, dma((2, 4)), dma((2, 4)), dma, dma, dma, dma,
        ],
        compiler_params=pltpu.CompilerParams(
            collective_id=0, has_side_effects=True, vmem_limit_bytes=48 * 1024 * 1024
        ),
        cost_estimate=pl.CostEstimate(flops=4 * 10**9, bytes_accessed=8 * 2**20,
                                      transcendentals=2 * 2**20),
    )(rows, key_rows, value_rows, info)

    def to_rows(array):
        return array.transpose(1, 2, 3, 0, 4, 5).reshape(128, HEADS * HEAD_DIM)

    lse_rows = lse[..., :16].transpose(1, 3, 0, 2).reshape(128, HEADS)
    return to_rows(out[:, :, :, 0]), lse_rows, to_rows(out[:, :, :, 1])


def solution(mesh):
    in_specs = (
        P(("dp", "ctx"), None),
        P(("dp", "ctx"), None),
        P(("dp", "ctx"), None),
        P(("dp", "ctx"), None),
        P("dp", None),
        P("dp", "ctx", None, None),
    )
    out_specs = (P(("dp", "ctx"), None), P(("dp", "ctx"), None), P(("dp", "ctx"), None))
    return jax.shard_map(local, mesh=mesh, in_specs=in_specs, out_specs=out_specs, check_vma=False)
```

time: 262 us -> 111 us (0.42); the launches traced: 257 us -> 111 us
  waiting for transfers between devices: 114 us -> 0 us
  Pallas kernels: 0 us -> 99.2 us
  starting transfers between devices: 52 us -> 0 us
  matrix products: 35.8 us -> 0 us
  local copies, waits for them, and re-layouts: 36.3 us -> 9.11 us
  between operations: 14.5 us -> 0.79 us
  other arithmetic: 4.81 us -> 1.73 us
    pallas_call x0 -> x1, Pallas kernels: none -> 99.2 us  [local(): pl.pallas_call(kernel, out_shape=(jax.ShapeDtypeStruct((KV_HEADS, NZ, NY,...]
    all_to_all x5 -> x0, waiting for transfers between devices: 69.6 us -> none  [the longest x1 23.4 us: local(): lax.all_to_all(out_send, 'dp', split_axis=0, concat_axis=0, tiled=True)]
    all_to_all x5 -> x0, starting transfers between devices: 51.9 us -> none  [the longest x1 17.3 us: local(): lax.all_to_all(outgoing[0], 'dp', split_axis=0, concat_axis=0, tiled=True)]
    all_gather x2 -> x0, waiting for transfers between devices: 42.7 us -> none  [the longest x1 28.7 us: local(): lax.all_gather(value_rows, 'ctx', axis=0, tiled=True)]
    dot_general x24 -> x0, matrix products: 35.8 us -> none  [the longest x8 17 us: local(): jnp.einsum('hnk,kd->nhd', score_grad, key_head, preferred_element_type=jn...]
    slice x9 -> x0, local copies, waits for them, and re-layouts: 19 us -> none  [the longest x1 6.39 us: local(): rows_grad = grad_heads[lower:lower + sub_rows]]
    reshape x8 -> x6, local copies, waits for them, and re-layouts: 11.3 us -> 4.58 us  [the longest x2 2.55 us: to_rows(): return array.transpose(1, 2, 3, 0, 4, 5).reshape(128, HEADS * HEAD_DIM)]
    reduce_sum x5 -> x1, other arithmetic: 2.86 us -> 0.11 us  [local(): marks = jnp.sum(jnp.where(chosen[:, :, None], parts[None], 0.0), axis=1)]
  transfers between devices with their start and end apart: 7 -> 0, of which waited for: 6 -> 0; matrix products, arithmetic and copies ran while one was open for 11% -> 0% of each run, Pallas kernels for 0% -> 0%
where the time goes in v1:
time: 111 us
  Pallas kernels  99.2 us (89%)
  local copies, waits for them, and re-layouts  9.11 us (8%)
  other arithmetic  1.73 us (2%)
    pallas_call x1, Pallas kernels, local(): pl.pallas_call(kernel, out_shape=(jax.ShapeDtypeStruct((KV_HEADS, NZ, NY,...  99.2 us
    reshape x2, local copies, waits for them, and re-layouts, to_rows(): return array.transpose(1, 2, 3, 0, 4, 5).reshape(128, HEADS * HEAD_DIM)  2.55 us
    unnamed x8, local copies, waits for them, and re-layouts  2.53 us

profile of v1, /device:TPU:1, one launch (start us, length us, event | category | flops | bytes accessed | tf_op | source)
XLA Modules:
  0.0 110.8 jit_solution(3332152737879071825)
XLA Ops:
  0.7 0.1 iota_compare_fusion
  0.8 0.9 reduce_window_sum.11
  1.6 0.8 le.16
  2.4 0.4 select_reduce_fusion
  2.8 0.8 reshape.287
  3.6 0.1 copy.36
  3.7 0.1 copy.37
  3.8 0.1 select_reduce_fusion.1
  3.9 0.1 convert_element_type.24
  4.0 0.0 copy-start.2
  4.0 1.5 %copy.43 = bf16[16,8,32,128]{3,2,1,0:T(8,128)(2,1)S(1)} copy(bf16[16,8,32,128]{3,1,2,0:T(8,128)(2,1)} %bitcast.44) | data formatting | bytes 2097152
  5.5 0.3 copy.28
  5.8 0.0 copy-done.2
  5.8 0.2 copy.44
  6.1 0.3 copy.29
  6.3 0.0 copy-start
  6.4 0.0 copy-start.1
  6.4 0.2 pad_maximum_fusion.rows
  6.6 0.7 copy-done
  7.3 0.1 copy-done.1
  7.3 99.2 %shard_map.85 = (bf16[4,8,8,2,2,8,128]{6,5,4,3,2,1,0:T(8,128)(2,1)S(1)}, f32[4,8,8,128]{3,2,1,0:T(8,128)S(1)}) custom-call(bf16[32,2,16,8,128]{4,3,2,1,0:T(8,128)(2,1)S(1)} %pad_maximum_fusion.rows, bf16[128,512]{1,0:T(8,128)(2,1)S(1)} %copy-done, bf16[128,512]{1,0:T(8,128)(2,1)S(1)} %copy-done.1, bf16[2,16,128]{2,1,0:T(8,128)(2,1)S(1)} %broadcast_bitcast_fusion.info), custom_call_target="tpu_custom_call" | custom-call | flops 4000000000 | bytes 8388608 | tf_op jit(solution)/shard_map/pallas_call | solution.py:285
  106.6 0.4 slice_bitcast_fusion
  107.0 0.3 copy.40
  107.3 1.3 %reshape.290 = bf16[128,4096]{1,0:T(8,128)(2,1)} reshape(bf16[8,8,2,4,8,128]{5,4,3,2,1,0:T(8,128)(2,1)S(1)} %copy.40) | data formatting | bytes 2097152 | tf_op jit(solution)/shard_map/reshape | solution.py:308
  108.6 0.7 reshape.289
  109.3 0.3 copy.38
  109.6 1.3 %reshape.288 = bf16[128,4096]{1,0:T(8,128)(2,1)} reshape(bf16[8,8,2,4,8,128]{5,4,3,2,1,0:T(8,128)(2,1)S(1)} %copy.38) | data formatting | bytes 2097152 | tf_op jit(solution)/shard_map/reshape | solution.py:308
  (7 shorter events, 0.1 us)
Async XLA Ops:
  4.0 1.8 %copy-start.2 = (bf16[128,4096]{1,0:T(8,128)(2,1)S(1)}, bf16[128,4096]{1,0:T(8,128)(2,1)}, u32[]{:S(2)}) copy-start(bf16[128,4096]{1,0:T(8,128)(2,1)} %param.9) | copy-start | bytes 3145732
  6.3 0.9 copy-start
  6.4 1.0 copy-start.1

commit v2 on v1

v2 whole, which is shorter than its diff:
```python
import functools
import math

import jax
import jax.numpy as jnp
from jax import lax
from jax.experimental import pallas as pl
from jax.experimental.pallas import tpu as pltpu
from jax.sharding import PartitionSpec as P

HEAD_DIM = 128
HEADS = 32
KV_HEADS = 4
GROUP = HEADS // KV_HEADS
SUBS = 2
NZ = 8
NY = 8
NX = 4
NCTX = 8
SLOTS = 32
HALF = 64
SEQ = 512
PLACES = NY
TILES = 4 * PLACES + 1
EARLY = 3
KV_ROWS = 272
NEG_FILL = -1e30
MESH = pl.DeviceIdType.MESH


def z_step(e, core):
    return e - 1 - 4 * core * (e // 3)


def rank(distance):
    return jnp.where(distance <= 4, jnp.maximum(2 * distance - 1, 0), 16 - 2 * distance)


def kernel(queries, grads, keys, values, lengths, positions, out,
           rows, kv_out, kv, got, res, lse, second,
           row_send, row_recv, kva_send, kvb_send, kv_recv, ring_send, ring_recv,
           res_send, res_recv):
    dp = lax.axis_index("dp")
    ctx = lax.axis_index("ctx")
    z, y = lax.div(dp, NY), lax.rem(dp, NY)
    x, core = lax.div(ctx, 2), lax.rem(ctx, 2)
    right = z * NY + lax.rem(y + 1, NY)
    left = z * NY + lax.rem(y + NY - 1, NY)

    def at_z(step):
        return lax.rem(z + step + NZ, NZ)

    def at_ctx(x_step, core_step):
        return lax.rem(x + x_step, NX) * 2 + lax.rem(core + core_step, 2)

    barrier = pltpu.get_barrier_semaphore()
    line = [(at_z(step) * NY + y, ctx) for step in (1, -1, 2, -2, 4)]
    near = [(dp, at_ctx(x_step, core_step)) for x_step in range(NX) for core_step in range(2)
            if x_step or core_step]
    for dev in line + near + [(left, ctx), (right, ctx)]:
        pl.semaphore_signal(barrier, inc=1, device_id=dev, device_id_type=MESH)

    places = [rank(lax.rem(y0 - y + NY, NY)) for y0 in range(NY)]

    def order_rows(home, carry):
        for head in range(KV_HEADS):
            for which, source in enumerate((queries, grads)):
                block = source[pl.ds(pl.multiple_of(home * 16, 16), 16),
                               head * GROUP * HEAD_DIM:(head + 1) * GROUP * HEAD_DIM]
                block = block.reshape(16, GROUP, HEAD_DIM)
                for y0 in range(NY):
                    rows[head * NZ + home, places[y0], which] = block[2 * y0:2 * y0 + 2]
        return carry

    pos = positions[...]
    spot = lax.broadcasted_iota(jnp.int32, (8, HALF), 0)
    first_rows = []
    for s in range(SUBS):
        line_pos = pos[s:s + 1, :]
        first = jnp.zeros_like(line_pos)
        end = jnp.int32(0)
        for doc in range(8):
            end = end + lengths[s, doc]
            first = jnp.where(line_pos >= end, end, first)
        first_rows.append(first)
    table = jnp.zeros((8, HALF), jnp.int32)
    for s in range(SUBS):
        for part, line_value in enumerate((pos[s:s + 1, :], first_rows[s])):
            high = lax.shift_right_logical(line_value, 4)
            table = jnp.where(spot == s * 4 + part * 2, high, table)
            table = jnp.where(spot == s * 4 + part * 2 + 1, line_value - high * 16, table)
    table = table.astype(jnp.float32).astype(jnp.bfloat16)
    lane8 = lax.broadcasted_iota(jnp.int32, (8, 128), 1)
    row8 = lax.broadcasted_iota(jnp.int32, (8, 128), 0)
    lane64 = lax.broadcasted_iota(jnp.int32, (HALF, 128), 1)
    row64 = lax.broadcasted_iota(jnp.int32, (HALF, 128), 0)
    wanted = lax.rem(lax.div(lane8, 32), 2) * 4 + lax.rem(lane8, 4)

    for copy in range(2):
        marks = []
        for e_hi in range(2):
            low, high = [at_z(4 * copy + z_step(2 * e_hi + e_lo, core)) for e_lo in range(2)]
            source = jnp.where(lane64 < 64, low, high) * NY + lax.rem(lax.div(lane64, 4), NY)
            pick_rows = (row64 == source).astype(jnp.float32).astype(jnp.bfloat16)
            found = jnp.dot(table, pick_rows, preferred_element_type=jnp.float32)
            found = jnp.sum(jnp.where(row8 == wanted, found, 0.0), axis=0, keepdims=True)
            marks.append(jnp.broadcast_to(found, (GROUP, 128)))
        marks = jnp.concatenate(marks, axis=0).astype(jnp.bfloat16)
        for head in range(KV_HEADS):
            cols = slice(head * HEAD_DIM, (head + 1) * HEAD_DIM)
            kv_out[copy, head, 0:128] = keys[:, cols]
            kv_out[copy, head, 128:256] = values[:, cols]
            kv_out[copy, head, 256:272] = marks

    lax.fori_loop(0, NZ, order_rows, 0)

    pl.semaphore_wait(barrier, len(line) + len(near) + 2)
    for dev in line:
        pl.semaphore_signal(second, inc=1, device_id=dev, device_id_type=MESH)
    pl.semaphore_wait(second, len(line))

    def remote(src, dst, send, recv, dev):
        return pltpu.make_async_remote_copy(src_ref=src, dst_ref=dst, send_sem=send, recv_sem=recv,
                                            device_id=dev, device_id_type=MESH)

    def wait_bytes(ref, sem):
        pltpu.make_async_copy(ref, ref, sem).wait()

    here = kv.at[y, ctx]
    for x_step in (1, 3, 2):
        head = lax.rem(x + x_step, NX)
        remote(kv_out.at[0, head], here, kva_send, kv_recv, (dp, head * 2)).start()

    @pl.when(core == 0)
    def _():
        pltpu.make_async_copy(kv_out.at[0, x], here, kv_recv).start()

    @pl.when(core != 0)
    def _():
        remote(kv_out.at[0, x], here, kva_send, kv_recv, (dp, x * 2)).start()

    far = at_z(4) * NY + y
    for x_step in (1, 3, 2, 0):
        head = lax.rem(x + x_step, NX)
        remote(kv_out.at[1, head], here, kvb_send, kv_recv, (far, head * 2 + 1)).start()

    def send_rows(part):
        ranks = pl.ds(0, EARLY) if part == 0 else pl.ds(EARLY, PLACES - EARLY)
        for e in (0, 2, 3, 1):
            server_z = at_z(-z_step(e, core))
            for other in range(2):
                copy = lax.rem(core + other, 2)
                home = lax.rem(server_z + 4 * copy, NZ)
                for x_step in (1, 3, 2, 0):
                    head = lax.rem(x + x_step, NX)
                    src = rows.at[head * NZ + home, ranks]
                    dst = got.at[(e % 2) * 16 + ctx * 2 + e // 2, ranks]
                    if e == 1 and other == 0 and x_step == 0:
                        pltpu.make_async_copy(src, dst, row_recv.at[part]).start()
                    else:
                        remote(src, dst, row_send.at[part], row_recv.at[part],
                               (server_z * NY + y, head * 2 + copy)).start()

    def ring(step):
        from_left = kv.at[lax.rem(y - step + NY, NY)]
        from_right = kv.at[lax.rem(y + step, NY)]
        if step == 3:
            from_left = from_left.at[pl.ds(0, 4)]
            from_right = from_right.at[pl.ds(4, 4)]
        return (remote(from_left, from_left, ring_send.at[0, step], ring_recv.at[0, step], (right, ctx)),
                remote(from_right, from_right, ring_send.at[1, step], ring_recv.at[1, step], (left, ctx)))

    def ring_start(step):
        for copy in ring(step):
            copy.start()

    def ring_arrived(step):
        from_left = kv.at[lax.rem(y - step - 1 + NY, NY)]
        from_right = kv.at[lax.rem(y + step + 1, NY)]
        if step == 3:
            from_left = from_left.at[pl.ds(0, 4)]
            from_right = from_right.at[pl.ds(4, 4)]
        wait_bytes(from_left, ring_recv.at[0, step])
        wait_bytes(from_right, ring_recv.at[1, step])

    send_rows(0)

    @pl.when(core == 0)
    def _():
        wait_bytes(kv.at[y], kv_recv)
        ring_start(0)

    send_rows(1)

    @pl.when(core != 0)
    def _():
        wait_bytes(kv.at[y], kv_recv)
        ring_start(0)

    scale = 1.0 / math.sqrt(HEAD_DIM)
    to_log2 = scale * math.log2(math.e)
    lane = lax.broadcasted_iota(jnp.int32, (128, 128), 0)
    key_pos = lax.broadcasted_iota(jnp.int32, (256, SEQ), 1).astype(jnp.float32)
    lse_lane = lax.broadcasted_iota(jnp.int32, (256, 128), 1)
    server_home = at_z(4 * core)

    def pick(base):
        return jnp.where(lane == base, 16.0, jnp.where(lane == base + 1, 1.0, 0.0)).astype(jnp.bfloat16)

    def dot(a, b, dims):
        return lax.dot_general(a, b, (dims, ((), ())), preferred_element_type=jnp.float32)

    def one_sequence(n, y0, s):
        q = got[:, n, 0, s].reshape(256, HEAD_DIM)
        g = got[:, n, 1, s].reshape(256, HEAD_DIM)
        k = kv[y0, :, pl.ds(pl.multiple_of(s * HALF, HALF), HALF), :].reshape(SEQ, HEAD_DIM)
        v = kv[y0, :, pl.ds(pl.multiple_of(128 + s * HALF, HALF), HALF), :].reshape(SEQ, HEAD_DIM)
        marks = kv[y0, :, pl.ds(256, 16), :].reshape(128, 128)
        bounds = []
        for which in range(2):
            halves = [dot(marks, pick(e_lo * 64 + s * 32 + y * 4 + which * 2), ((1,), (0,)))
                      for e_lo in range(2)]
            whole = jnp.concatenate(halves, axis=0)
            bounds.append(jnp.concatenate([whole] * 4, axis=1))
        visible = jnp.logical_and(key_pos <= bounds[0], key_pos >= bounds[1])
        scores = jnp.where(visible, dot(q, k, ((1,), (1,))) * to_log2, NEG_FILL)
        top = jnp.max(scores, axis=1, keepdims=True)
        p = jnp.exp2(scores - top)
        total = jnp.sum(p, axis=1, keepdims=True)
        inverse = 1.0 / total
        att = (dot(p.astype(jnp.bfloat16), v, ((1,), (0,))) * inverse).astype(jnp.bfloat16)
        delta = jnp.sum(g.astype(jnp.float32) * att.astype(jnp.float32), axis=1, keepdims=True)
        grad = dot(g, v, ((1,), (1,)))
        ds = (p * (grad - delta)).astype(jnp.bfloat16)
        dq = (dot(ds, k, ((1,), (0,))) * (inverse * scale)).astype(jnp.bfloat16)
        res[:, n * 4 + s] = att.reshape(SLOTS, GROUP, HEAD_DIM)
        res[:, n * 4 + 2 + s] = dq.reshape(SLOTS, GROUP, HEAD_DIM)
        left_over = (top + jnp.log2(total)) * math.log(2.0)
        kept = lse[...]
        for part in range(3):
            term = left_over.astype(jnp.bfloat16).astype(jnp.float32)
            left_over = left_over - term
            kept = jnp.where(lse_lane == part * 16 + y0 * SUBS + s, term, kept)
        lse[...] = kept

    def serve(n, carry):
        y0 = lax.rem(y + lax.div(n + 1, 2) * (2 * lax.rem(n, 2) - 1) + NY, NY)

        def sub(s, inner):
            one_sequence(n, y0, s)
            return inner

        return lax.fori_loop(0, SUBS, sub, carry)

    def give(lower, upper):
        tiles = pl.ds(lower * 4, (upper - lower) * 4 + (1 if upper == PLACES else 0))
        dst = out.at[x, server_home, tiles]
        for e in (0, 2, 3, 1):
            for other in range(2):
                home_core = lax.rem(core + other, 2)
                home_z = at_z(z_step(e, home_core))
                for x_step in (1, 3, 2, 0):
                    home_ctx = lax.rem(x + x_step, NX) * 2 + home_core
                    src = res.at[(e % 2) * 16 + home_ctx * 2 + e // 2, tiles]
                    if e == 1 and other == 0 and x_step == 0:
                        pltpu.make_async_copy(src, dst, res_recv).start()
                    else:
                        remote(src, dst, res_send, res_recv, (home_z * NY + y, home_ctx)).start()

    lse[...] = jnp.zeros_like(lse)
    ring_arrived(0)
    ring_start(1)
    wait_bytes(got.at[:, pl.ds(0, EARLY)], row_recv.at[0])
    lax.fori_loop(0, 3, serve, 0)
    give(0, 3)
    ring_arrived(1)
    ring_start(2)
    wait_bytes(got.at[:, pl.ds(EARLY, PLACES - EARLY)], row_recv.at[1])
    lax.fori_loop(3, 5, serve, 0)
    give(3, 5)
    ring_arrived(2)
    ring_start(3)
    lax.fori_loop(5, 7, serve, 0)
    give(5, 7)
    ring_arrived(3)
    lax.fori_loop(7, 8, serve, 0)
    res[:, 4 * PLACES] = lse[...].astype(jnp.bfloat16).reshape(SLOTS, GROUP, 128)
    give(7, 8)

    sent = pl.ds(0, SLOTS - 1)
    wait_bytes(rows.at[sent, pl.ds(0, EARLY)], row_send.at[0])
    wait_bytes(rows.at[sent, pl.ds(EARLY, PLACES - EARLY)], row_send.at[1])
    wait_bytes(kv.at[0, pl.ds(0, 4)], kvb_send)

    @pl.when(core == 0)
    def _():
        wait_bytes(kv.at[0, pl.ds(0, 3)], kva_send)

    @pl.when(core != 0)
    def _():
        wait_bytes(kv.at[0, pl.ds(0, 4)], kva_send)

    for step in range(4):
        for copy in ring(step):
            copy.wait_send()
    wait_bytes(res.at[sent], res_send)
    wait_bytes(out, res_recv)


def order_results(got, attended, lse, grad):
    home = pl.program_id(0)
    y = lax.rem(lax.axis_index("dp"), NY)
    for head in range(KV_HEADS):
        cols = slice(head * GROUP * HEAD_DIM, (head + 1) * GROUP * HEAD_DIM)
        for which, result in enumerate((attended, grad)):
            pairs = [got[head, 0, pl.ds(4 * rank(lax.rem(y0 - y + NY, NY)) + 2 * which, 2)]
                     for y0 in range(NY)]
            result[:, cols] = jnp.concatenate(pairs, axis=0).reshape(16, GROUP * HEAD_DIM)
    terms = got[:, 0, 4 * PLACES].reshape(HEADS, 128).astype(jnp.float32)
    total = terms + pltpu.roll(terms, 112, 1) + pltpu.roll(terms, 96, 1)
    lane = lax.broadcasted_iota(jnp.int32, (HEADS, 128), 1)
    total = pltpu.roll(jnp.where(lane < 16, total, 0.0), home * 16, 1)

    @pl.when(home == 0)
    def _():
        lse[...] = total

    @pl.when(home != 0)
    def _():
        lse[...] = lse[...] + total


def local(queries, key_rows, value_rows, out_grad, doc_lengths, served_positions):
    bf16 = jnp.bfloat16
    dma = pltpu.SemaphoreType.DMA
    vmem = pl.BlockSpec(memory_space=pltpu.VMEM)
    result = pl.pallas_call(
        kernel,
        out_shape=jax.ShapeDtypeStruct((KV_HEADS, NZ, TILES, GROUP, HEAD_DIM), bf16),
        in_specs=[vmem, vmem, vmem, vmem, pl.BlockSpec(memory_space=pltpu.SMEM), vmem],
        out_specs=pl.BlockSpec(memory_space=pl.ANY),
        scratch_shapes=[
            pltpu.VMEM((SLOTS, PLACES, 2, SUBS, GROUP, HEAD_DIM), bf16),
            pltpu.VMEM((2, KV_HEADS, KV_ROWS, HEAD_DIM), bf16),
            pltpu.VMEM((NY, NCTX, KV_ROWS, HEAD_DIM), bf16),
            pltpu.VMEM((SLOTS, PLACES, 2, SUBS, GROUP, HEAD_DIM), bf16),
            pltpu.VMEM((SLOTS, TILES, GROUP, HEAD_DIM), bf16),
            pltpu.VMEM((SLOTS * GROUP, 128), jnp.float32),
            pltpu.SemaphoreType.REGULAR,
            dma((2,)), dma((2,)), dma, dma, dma, dma((2, 4)), dma((2, 4)), dma, dma,
        ],
        compiler_params=pltpu.CompilerParams(
            collective_id=0, has_side_effects=True, vmem_limit_bytes=48 * 1024 * 1024
        ),
        cost_estimate=pl.CostEstimate(flops=4 * 10**9, bytes_accessed=8 * 2**20,
                                      transcendentals=2 * 2**20),
    )(queries, out_grad, key_rows, value_rows, doc_lengths,
      served_positions.reshape(NZ * NY, SUBS).T)

    wide = HEADS * HEAD_DIM
    attended, lse, grad = pl.pallas_call(
        order_results,
        grid=(NZ,),
        out_shape=(
            jax.ShapeDtypeStruct((NZ * 16, wide), bf16),
            jax.ShapeDtypeStruct((HEADS, 128), jnp.float32),
            jax.ShapeDtypeStruct((NZ * 16, wide), bf16),
        ),
        in_specs=[pl.BlockSpec((KV_HEADS, 1, TILES, GROUP, HEAD_DIM), lambda i: (0, i, 0, 0, 0))],
        out_specs=(
            pl.BlockSpec((16, wide), lambda i: (i, 0)),
            pl.BlockSpec((HEADS, 128), lambda i: (0, 0)),
            pl.BlockSpec((16, wide), lambda i: (i, 0)),
        ),
        cost_estimate=pl.CostEstimate(flops=0, bytes_accessed=4 * 2**20, transcendentals=0),
    )(result)
    return attended, lse.T, grad


def solution(mesh):
    in_specs = (
        P(("dp", "ctx"), None),
        P(("dp", "ctx"), None),
        P(("dp", "ctx"), None),
        P(("dp", "ctx"), None),
        P("dp", None),
        P("dp", "ctx", None, None),
    )
    out_specs = (P(("dp", "ctx"), None), P(("dp", "ctx"), None), P(("dp", "ctx"), None))
    return jax.shard_map(local, mesh=mesh, in_specs=in_specs, out_specs=out_specs, check_vma=False)
```

time: 111 us -> 99.1 us (0.89)
  Pallas kernels: 99.2 us -> 91.1 us
  local copies, waits for them, and re-layouts: 9.11 us -> 6.95 us
  other arithmetic: 1.73 us -> 0 us
    pallas_call x1 -> x2, Pallas kernels: 99.2 us -> 91.1 us  [the longest x1 84.9 us: local(): pl.pallas_call(kernel, out_shape=jax.ShapeDtypeStruct((KV_HEADS, NZ, TILE...]
    reshape x6 -> x0, local copies, waits for them, and re-layouts: 4.58 us -> none  [the longest x2 2.55 us: to_rows(): return array.transpose(1, 2, 3, 0, 4, 5).reshape(128, HEADS * HEAD_DIM)]
    unnamed x8 -> x14, local copies, waits for them, and re-layouts: 2.53 us -> 6.95 us
where the time goes in v2:
time: 99.1 us; the launch traced here: 98.8 us
  Pallas kernels  91.1 us (92%)
  local copies, waits for them, and re-layouts  6.95 us (7%)
    pallas_call x1, Pallas kernels, local(): pl.pallas_call(kernel, out_shape=jax.ShapeDtypeStruct((KV_HEADS, NZ, TILE...  84.9 us
    unnamed x14, local copies, waits for them, and re-layouts  6.95 us
    pallas_call x1, Pallas kernels, local(): pl.pallas_call(order_results, grid=(NZ,), out_shape=(jax.ShapeDtypeStruct...  6.29 us

profile of v2, /device:TPU:1, one launch (start us, length us, event | category | flops | bytes accessed | tf_op | source)
XLA Modules:
  0.0 98.8 jit_solution(890882109067439315)
XLA Ops:
  0.6 0.0 copy-start.1
  0.6 1.2 %copy-done.1 = bf16[128,4096]{1,0:T(8,128)(2,1)S(1)} copy-done((bf16[128,4096]{1,0:T(8,128)(2,1)S(1)}, bf16[128,4096]{1,0:T(8,128)(2,1)}, u32[]{:S(2)}) %copy-start.1) | copy-done | bytes 1048600
  1.9 0.0 copy-start.2
  1.9 1.2 %copy-done.2 = bf16[128,4096]{1,0:T(8,128)(2,1)S(1)} copy-done((bf16[128,4096]{1,0:T(8,128)(2,1)S(1)}, bf16[128,4096]{1,0:T(8,128)(2,1)}, u32[]{:S(2)}) %copy-start.2) | copy-done | bytes 1048600
  3.1 0.0 copy-start.3
  3.1 0.9 copy-done.3
  4.0 0.0 copy-start.4
  4.0 0.9 copy-done.4
  4.9 0.0 copy-start.5
  4.9 0.7 copy-done.5
  5.6 0.0 copy-start.6
  5.6 0.7 copy-done.6
  6.3 84.9 %shard_map.85.got = bf16[4,8,33,8,128]{4,3,2,1,0:T(8,128)(2,1)S(1)} custom-call(bf16[128,4096]{1,0:T(8,128)(2,1)S(1)} %copy-done.1, bf16[128,4096]{1,0:T(8,128)(2,1)S(1)} %copy-done.2, bf16[128,512]{1,0:T(8,128)(2,1)S(1)} %copy-done.3, bf16[128,512]{1,0:T(8,128)(2,1)S(1)} %copy-done.4, s32[2,8]{1,0:T(2,128)S(1)} %copy-done.5, s32[2,64]{1,0:T(2,128)S(1)} %bitcast.4), custom_call_target="tpu_custom_call" | custom-call | flops 4000000000 | bytes 8388608 | tf_op jit(solution)/shard_map/pallas_call | solution.py:337
  91.1 0.0 copy-start
  91.1 1.3 %copy-done = bf16[4,8,33,8,128]{4,3,2,1,0:T(8,128)(2,1)} copy-done((bf16[4,8,33,8,128]{4,3,2,1,0:T(8,128)(2,1)}, bf16[4,8,33,8,128]{4,3,2,1,0:T(8,128)(2,1)S(1)}, u32[]{:S(2)}) %copy-start) | copy-done | bytes 2162712
  92.5 6.3 %shard_map.86 = (bf16[128,4096]{1,0:T(8,128)(2,1)}, f32[32,128]{1,0:T(8,128)}, bf16[128,4096]{1,0:T(8,128)(2,1)}) custom-call(bf16[4,8,33,8,128]{4,3,2,1,0:T(8,128)(2,1)} %copy-done), custom_call_target="tpu_custom_call" | custom-call | bytes 4194304 | tf_op jit(solution)/shard_map/pallas_call | solution.py:361
Async XLA Ops:
  0.6 1.2 %copy-start.1 = (bf16[128,4096]{1,0:T(8,128)(2,1)S(1)}, bf16[128,4096]{1,0:T(8,128)(2,1)}, u32[]{:S(2)}) copy-start(bf16[128,4096]{1,0:T(8,128)(2,1)} %queries.1) | copy-start | bytes 3145732
  1.9 1.2 %copy-start.2 = (bf16[128,4096]{1,0:T(8,128)(2,1)S(1)}, bf16[128,4096]{1,0:T(8,128)(2,1)}, u32[]{:S(2)}) copy-start(bf16[128,4096]{1,0:T(8,128)(2,1)} %grads.1) | copy-start | bytes 3145732
  3.1 0.9 copy-start.3
  4.0 0.9 copy-start.4
  4.9 0.7 copy-start.5
  5.6 0.7 copy-start.6
  91.1 1.3 %copy-start = (bf16[4,8,33,8,128]{4,3,2,1,0:T(8,128)(2,1)}, bf16[4,8,33,8,128]{4,3,2,1,0:T(8,128)(2,1)S(1)}, u32[]{:S(2)}) copy-start(bf16[4,8,33,8,128]{4,3,2,1,0:T(8,128)(2,1)S(1)} %shard_map.85.got) | copy-start | bytes 6488068

commit v3 on v2

v3 whole, which is shorter than its diff:
```python
import functools
import math

import jax
import jax.numpy as jnp
from jax import lax
from jax.experimental import pallas as pl
from jax.experimental.pallas import tpu as pltpu
from jax.sharding import PartitionSpec as P

HEAD_DIM = 128
HEADS = 32
KV_HEADS = 4
GROUP = HEADS // KV_HEADS
SUBS = 2
NZ = 8
NY = 8
NX = 4
NCTX = 8
SLOTS = 32
HALF = 64
SEQ = 512
PLACES = NY
TILES = 4 * PLACES + 1
EARLY = 3
STEPS = (0, 1, 3, 2)
KV_ROWS = 272
NEG_FILL = -1e30
MESH = pl.DeviceIdType.MESH


def y_step(e, core):
    return e - 1 - 4 * core * (e // 3)


def rank(distance):
    return jnp.where(distance <= 4, jnp.maximum(2 * distance - 1, 0), 16 - 2 * distance)


def kernel(queries, grads, keys, values, lengths, positions, out,
           query_in, grad_in, key_in, value_in, lengths_in, positions_in,
           rows, kv_out, kv, got, res, lse, second,
           load, small_load, row_send, row_recv, kva_send, kvb_send, kv_recv, ring_send, ring_recv,
           res_send, res_recv):
    dp = lax.axis_index("dp")
    ctx = lax.axis_index("ctx")
    z, y = lax.div(dp, NY), lax.rem(dp, NY)
    x, core = lax.div(ctx, 2), lax.rem(ctx, 2)
    right = lax.rem(z + 1, NZ) * NY + y
    left = lax.rem(z + NZ - 1, NZ) * NY + y

    def at_y(step):
        return lax.rem(y + step + NY, NY)

    def at_ctx(x_step, core_step):
        return lax.rem(x + x_step, NX) * 2 + lax.rem(core + core_step, 2)

    barrier = pltpu.get_barrier_semaphore()
    line = [(z * NY + at_y(step), ctx) for step in (1, -1, 2, -2, 4)]
    near = [(dp, at_ctx(x_step, core_step)) for x_step in range(NX) for core_step in range(2)
            if x_step or core_step]
    for dev in line + near + [(left, ctx), (right, ctx)]:
        pl.semaphore_signal(barrier, inc=1, device_id=dev, device_id_type=MESH)

    def load_rows(home_z, which):
        block = pl.ds(home_z * 16, 16)
        source, target = ((queries, query_in), (grads, grad_in))[which]
        return pltpu.make_async_copy(source.at[block], target.at[block], load.at[which, home_z])

    small = [pltpu.make_async_copy(source, target, small_load.at[i])
             for i, (source, target) in enumerate(((lengths, lengths_in), (positions, positions_in),
                                                   (keys, key_in), (values, value_in)))]
    for copy in small:
        copy.start()
    for home_z in range(NZ):
        for which in range(2):
            load_rows(home_z, which).start()
    for copy in small:
        copy.wait()

    def order_rows(home_z, carry):
        place = rank(lax.rem(home_z - z + NZ, NZ))
        lines = pl.ds(pl.multiple_of(home_z * 16, 16), 16)
        for which, source in enumerate((query_in, grad_in)):
            load_rows(home_z, which).wait()
            for head in range(KV_HEADS):
                block = source[lines, head * GROUP * HEAD_DIM:(head + 1) * GROUP * HEAD_DIM]
                block = block.reshape(16, GROUP, HEAD_DIM)
                for home_y in range(NY):
                    rows[head * NY + home_y, place, which] = block[2 * home_y:2 * home_y + 2]
        return carry

    pos = positions_in[...]
    spans = lengths_in[...]
    doc_lane = lax.broadcasted_iota(jnp.int32, (SUBS, 8), 1)
    first = jnp.zeros_like(pos)
    for doc in range(8):
        end = jnp.sum(jnp.where(doc_lane <= doc, spans, 0), axis=1, keepdims=True)
        first = jnp.where(pos >= end, end, first)
    spot = lax.broadcasted_iota(jnp.int32, (8, HALF), 0)
    table = jnp.zeros((8, HALF), jnp.int32)
    for s in range(SUBS):
        for part, line_value in enumerate((pos[s:s + 1, :], first[s:s + 1, :])):
            high = lax.shift_right_logical(line_value, 4)
            table = jnp.where(spot == s * 4 + part * 2, high, table)
            table = jnp.where(spot == s * 4 + part * 2 + 1, line_value - high * 16, table)
    table = table.astype(jnp.float32).astype(jnp.bfloat16)
    lane8 = lax.broadcasted_iota(jnp.int32, (8, 128), 1)
    row8 = lax.broadcasted_iota(jnp.int32, (8, 128), 0)
    lane64 = lax.broadcasted_iota(jnp.int32, (HALF, 128), 1)
    row64 = lax.broadcasted_iota(jnp.int32, (HALF, 128), 0)
    wanted = lax.rem(lax.div(lane8, 32), 2) * 4 + lax.rem(lane8, 4)

    for copy in range(2):
        marks = []
        for e_hi in range(2):
            low, high = [at_y(4 * copy + y_step(2 * e_hi + e_lo, core)) for e_lo in range(2)]
            source = jnp.where(lane64 < 64, low, high) + lax.rem(lax.div(lane64, 4), NZ) * NY
            pick_rows = (row64 == source).astype(jnp.float32).astype(jnp.bfloat16)
            found = jnp.dot(table, pick_rows, preferred_element_type=jnp.float32)
            found = jnp.sum(jnp.where(row8 == wanted, found, 0.0), axis=0, keepdims=True)
            marks.append(jnp.broadcast_to(found, (GROUP, 128)))
        marks = jnp.concatenate(marks, axis=0).astype(jnp.bfloat16)
        for head in range(KV_HEADS):
            cols = slice(head * HEAD_DIM, (head + 1) * HEAD_DIM)
            kv_out[copy, head, 0:128] = key_in[:, cols]
            kv_out[copy, head, 128:256] = value_in[:, cols]
            kv_out[copy, head, 256:272] = marks

    lax.fori_loop(0, NZ, order_rows, 0)

    pl.semaphore_wait(barrier, len(line) + len(near) + 2)
    for dev in line:
        pl.semaphore_signal(second, inc=1, device_id=dev, device_id_type=MESH)
    pl.semaphore_wait(second, len(line))

    def remote(src, dst, send, recv, dev):
        return pltpu.make_async_remote_copy(src_ref=src, dst_ref=dst, send_sem=send, recv_sem=recv,
                                            device_id=dev, device_id_type=MESH)

    def wait_bytes(ref, sem):
        pltpu.make_async_copy(ref, ref, sem).wait()

    here = kv.at[z, ctx]
    arrived = kv_recv.at[x]

    @pl.when(core == 0)
    def _():
        pltpu.make_async_copy(kv_out.at[0, x], here, arrived).start()

    @pl.when(core != 0)
    def _():
        remote(kv_out.at[0, x], here, kva_send, arrived, (dp, x * 2)).start()

    far = z * NY + at_y(4)
    remote(kv_out.at[1, x], here, kvb_send, arrived, (far, x * 2 + 1)).start()
    for x_step in STEPS[1:]:
        head = lax.rem(x + x_step, NX)
        remote(kv_out.at[0, head], here, kva_send, arrived, (dp, head * 2)).start()
        remote(kv_out.at[1, head], here, kvb_send, arrived, (far, head * 2 + 1)).start()

    def send_rows(part, which_e):
        ranks = pl.ds(0, EARLY) if part == 0 else pl.ds(EARLY, PLACES - EARLY)
        for e in which_e:
            server_y = at_y(-y_step(e, core))
            for other in range(2):
                copy = lax.rem(core + other, 2)
                home = lax.rem(server_y + 4 * copy, NY)
                for x_step in (1, 3, 2, 0):
                    head = lax.rem(x + x_step, NX)
                    src = rows.at[head * NY + home, ranks]
                    dst = got.at[(e % 2) * 16 + ctx * 2 + e // 2, ranks]
                    if e == 1 and other == 0 and x_step == 0:
                        pltpu.make_async_copy(src, dst, row_recv.at[part]).start()
                    else:
                        remote(src, dst, row_send.at[part], row_recv.at[part],
                               (z * NY + server_y, head * 2 + copy)).start()

    def piece(chunk, i):
        return kv.at[chunk, pl.ds(lax.rem(x + STEPS[i], NX) * 2, 2)]

    def from_left(step):
        return lax.rem(z - step + NZ, NZ)

    def from_right(step):
        return lax.rem(z + step, NZ)

    def pieces(step, way):
        return range(NX) if step < 3 else range(2 * way, 2 * way + 2)

    def forward(step, i):
        if i in pieces(step, 0):
            block = piece(from_left(step), i)
            remote(block, block, ring_send.at[0, step], ring_recv.at[0, step, i], (right, ctx)).start()
        if i in pieces(step, 1):
            block = piece(from_right(step), i)
            remote(block, block, ring_send.at[1, step], ring_recv.at[1, step, i], (left, ctx)).start()

    def begin_ring(i):
        wait_bytes(piece(z, i), kv_recv.at[lax.rem(x + STEPS[i], NX)])
        forward(0, i)

    def pass_on(step):
        for i in range(NX):
            if i in pieces(step, 0):
                wait_bytes(piece(from_left(step + 1), i), ring_recv.at[0, step, i])
            if i in pieces(step, 1):
                wait_bytes(piece(from_right(step + 1), i), ring_recv.at[1, step, i])
            if step < 3:
                forward(step + 1, i)

    send_rows(0, (0, 2, 3, 1))
    begin_ring(0)
    send_rows(1, (0,))
    begin_ring(1)
    send_rows(1, (2,))
    begin_ring(2)
    send_rows(1, (3,))
    begin_ring(3)
    send_rows(1, (1,))

    scale = 1.0 / math.sqrt(HEAD_DIM)
    to_log2 = scale * math.log2(math.e)
    lane = lax.broadcasted_iota(jnp.int32, (128, 128), 0)
    key_pos = lax.broadcasted_iota(jnp.int32, (256, SEQ), 1).astype(jnp.float32)
    lse_lane = lax.broadcasted_iota(jnp.int32, (256, 128), 1)
    server_home = at_y(4 * core)

    def pick(base):
        return jnp.where(lane == base, 16.0, jnp.where(lane == base + 1, 1.0, 0.0)).astype(jnp.bfloat16)

    def dot(a, b, dims):
        return lax.dot_general(a, b, (dims, ((), ())), preferred_element_type=jnp.float32)

    def one_sequence(n, chunk, s):
        q = got[:, n, 0, s].reshape(256, HEAD_DIM)
        g = got[:, n, 1, s].reshape(256, HEAD_DIM)
        k = kv[chunk, :, pl.ds(pl.multiple_of(s * HALF, HALF), HALF), :].reshape(SEQ, HEAD_DIM)
        v = kv[chunk, :, pl.ds(pl.multiple_of(128 + s * HALF, HALF), HALF), :].reshape(SEQ, HEAD_DIM)
        marks = kv[chunk, :, pl.ds(256, 16), :].reshape(128, 128)
        bounds = []
        for which in range(2):
            halves = [dot(marks, pick(e_lo * 64 + s * 32 + z * 4 + which * 2), ((1,), (0,)))
                      for e_lo in range(2)]
            whole = jnp.concatenate(halves, axis=0)
            bounds.append(jnp.concatenate([whole] * 4, axis=1))
        visible = jnp.logical_and(key_pos <= bounds[0], key_pos >= bounds[1])
        scores = jnp.where(visible, dot(q, k, ((1,), (1,))) * to_log2, NEG_FILL)
        top = jnp.max(scores, axis=1, keepdims=True)
        p = jnp.exp2(scores - top)
        total = jnp.sum(p, axis=1, keepdims=True)
        inverse = 1.0 / total
        att = (dot(p.astype(jnp.bfloat16), v, ((1,), (0,))) * inverse).astype(jnp.bfloat16)
        delta = jnp.sum(g.astype(jnp.float32) * att.astype(jnp.float32), axis=1, keepdims=True)
        grad = dot(g, v, ((1,), (1,)))
        ds = (p * (grad - delta)).astype(jnp.bfloat16)
        dq = (dot(ds, k, ((1,), (0,))) * (inverse * scale)).astype(jnp.bfloat16)
        res[:, n * 4 + s] = att.reshape(SLOTS, GROUP, HEAD_DIM)
        res[:, n * 4 + 2 + s] = dq.reshape(SLOTS, GROUP, HEAD_DIM)
        left_over = (top + jnp.log2(total)) * math.log(2.0)
        kept = lse[...]
        for part in range(3):
            term = left_over.astype(jnp.bfloat16).astype(jnp.float32)
            left_over = left_over - term
            kept = jnp.where(lse_lane == part * 16 + chunk * SUBS + s, term, kept)
        lse[...] = kept

    def serve(n, carry):
        chunk = lax.rem(z + lax.div(n + 1, 2) * (2 * lax.rem(n, 2) - 1) + NZ, NZ)

        def sub(s, inner):
            one_sequence(n, chunk, s)
            return inner

        return lax.fori_loop(0, SUBS, sub, carry)

    def give(lower, upper):
        tiles = pl.ds(lower * 4, (upper - lower) * 4 + (1 if upper == PLACES else 0))
        dst = out.at[x, server_home, tiles]
        for e in (0, 2, 3, 1):
            for other in range(2):
                home_core = lax.rem(core + other, 2)
                home_y = at_y(y_step(e, home_core))
                for x_step in (1, 3, 2, 0):
                    home_ctx = lax.rem(x + x_step, NX) * 2 + home_core
                    src = res.at[(e % 2) * 16 + home_ctx * 2 + e // 2, tiles]
                    if e == 1 and other == 0 and x_step == 0:
                        pltpu.make_async_copy(src, dst, res_recv).start()
                    else:
                        remote(src, dst, res_send, res_recv, (z * NY + home_y, home_ctx)).start()

    lse[...] = jnp.zeros_like(lse)
    pass_on(0)
    wait_bytes(got.at[:, pl.ds(0, EARLY)], row_recv.at[0])
    lax.fori_loop(0, 3, serve, 0)
    give(0, 3)
    pass_on(1)
    wait_bytes(got.at[:, pl.ds(EARLY, PLACES - EARLY)], row_recv.at[1])
    lax.fori_loop(3, 5, serve, 0)
    give(3, 5)
    pass_on(2)
    lax.fori_loop(5, 7, serve, 0)
    give(5, 7)
    pass_on(3)
    lax.fori_loop(7, 8, serve, 0)
    res[:, 4 * PLACES] = lse[...].astype(jnp.bfloat16).reshape(SLOTS, GROUP, 128)
    give(7, 8)

    sent = pl.ds(0, SLOTS - 1)
    wait_bytes(rows.at[sent, pl.ds(0, EARLY)], row_send.at[0])
    wait_bytes(rows.at[sent, pl.ds(EARLY, PLACES - EARLY)], row_send.at[1])
    wait_bytes(kv.at[0, pl.ds(0, 4)], kvb_send)

    @pl.when(core == 0)
    def _():
        wait_bytes(kv.at[0, pl.ds(0, 3)], kva_send)

    @pl.when(core != 0)
    def _():
        wait_bytes(kv.at[0, pl.ds(0, 4)], kva_send)

    for step in range(4):
        for way in range(2):
            wait_bytes(kv.at[0] if step < 3 else kv.at[0, pl.ds(0, 4)], ring_send.at[way, step])
    wait_bytes(res.at[sent], res_send)
    wait_bytes(out, res_recv)


def order_results(got, attended, lse, grad, held, attended_rows, lse_rows, grad_rows,
                  load, store, lse_store):
    z = lax.div(lax.axis_index("dp"), NY)

    def load_part(n):
        tiles = pl.ds(4 * n, 4) if n < PLACES else pl.ds(4 * PLACES, 1)
        return pltpu.make_async_copy(got.at[:, :, tiles], held.at[:, :, tiles], load.at[n])

    def store_part(n, which):
        chunk = lax.rem(z + ((n + 1) // 2) * (2 * (n % 2) - 1) + NZ, NZ)
        lines = pl.ds(pl.multiple_of(chunk * 16, 16), 16)
        source, target = ((attended_rows, attended), (grad_rows, grad))[which]
        return lines, source, pltpu.make_async_copy(source.at[lines], target.at[lines], store.at[which, n])

    order = [PLACES] + list(range(PLACES))
    for n in order:
        load_part(n).start()
    load_part(PLACES).wait()
    column = lax.broadcasted_iota(jnp.int32, (128, 128), 1)
    source = lax.broadcasted_iota(jnp.int32, (128, 128), 0)
    target = lax.div(lax.rem(source, 16), 2) * 16 + lax.rem(source, 2)
    target = jnp.where(source < 48, target, -128)
    total = jnp.zeros((HEADS, 128), jnp.float32)
    for home_y in range(NY):
        terms = held[:, home_y, 4 * PLACES].reshape(HEADS, 128)
        place = (column == target + home_y * SUBS).astype(jnp.float32).astype(jnp.bfloat16)
        total = total + jnp.dot(terms, place, preferred_element_type=jnp.float32)
    lse_rows[...] = total
    lse_copy = pltpu.make_async_copy(lse_rows, lse, lse_store)
    lse_copy.start()
    for n in range(PLACES):
        load_part(n).wait()
        for which in range(2):
            lines, result, copy = store_part(n, which)
            for head in range(KV_HEADS):
                cols = slice(head * GROUP * HEAD_DIM, (head + 1) * GROUP * HEAD_DIM)
                block = held[head, :, 4 * n + 2 * which:4 * n + 2 * which + 2]
                result[lines, cols] = block.reshape(16, GROUP * HEAD_DIM)
            copy.start()
    for n in range(PLACES):
        for which in range(2):
            store_part(n, which)[2].wait()
    lse_copy.wait()


def local(queries, key_rows, value_rows, out_grad, doc_lengths, served_positions):
    bf16 = jnp.bfloat16
    dma = pltpu.SemaphoreType.DMA
    hbm = pl.BlockSpec(memory_space=pltpu.HBM)
    wide = HEADS * HEAD_DIM
    thin = KV_HEADS * HEAD_DIM
    result = pl.pallas_call(
        kernel,
        out_shape=jax.ShapeDtypeStruct((KV_HEADS, NY, TILES, GROUP, HEAD_DIM), bf16),
        in_specs=[hbm] * 6,
        out_specs=hbm,
        scratch_shapes=[
            pltpu.VMEM((NZ * 16, wide), bf16),
            pltpu.VMEM((NZ * 16, wide), bf16),
            pltpu.VMEM((128, thin), bf16),
            pltpu.VMEM((128, thin), bf16),
            pltpu.VMEM((SUBS, 8), jnp.int32),
            pltpu.VMEM((SUBS, HALF), jnp.int32),
            pltpu.VMEM((SLOTS, PLACES, 2, SUBS, GROUP, HEAD_DIM), bf16),
            pltpu.VMEM((2, KV_HEADS, KV_ROWS, HEAD_DIM), bf16),
            pltpu.VMEM((NZ, NCTX, KV_ROWS, HEAD_DIM), bf16),
            pltpu.VMEM((SLOTS, PLACES, 2, SUBS, GROUP, HEAD_DIM), bf16),
            pltpu.VMEM((SLOTS, TILES, GROUP, HEAD_DIM), bf16),
            pltpu.VMEM((SLOTS * GROUP, 128), jnp.float32),
            pltpu.SemaphoreType.REGULAR,
            dma((2, NZ)), dma((4,)), dma((2,)), dma((2,)), dma, dma, dma((NX,)),
            dma((2, 4)), dma((2, 4, NX)), dma, dma,
        ],
        compiler_params=pltpu.CompilerParams(
            collective_id=0, has_side_effects=True, vmem_limit_bytes=48 * 1024 * 1024
        ),
        cost_estimate=pl.CostEstimate(flops=4 * 10**9, bytes_accessed=8 * 2**20,
                                      transcendentals=2 * 2**20),
    )(queries, out_grad, key_rows, value_rows, doc_lengths,
      served_positions.reshape(NZ * NY, SUBS).T)

    attended, lse, grad = pl.pallas_call(
        order_results,
        out_shape=(
            jax.ShapeDtypeStruct((NZ * 16, wide), bf16),
            jax.ShapeDtypeStruct((HEADS, 128), jnp.float32),
            jax.ShapeDtypeStruct((NZ * 16, wide), bf16),
        ),
        in_specs=[hbm],
        out_specs=(hbm, hbm, hbm),
        scratch_shapes=[
            pltpu.VMEM((KV_HEADS, NY, TILES, GROUP, HEAD_DIM), bf16),
            pltpu.VMEM((NZ * 16, wide), bf16),
            pltpu.VMEM((HEADS, 128), jnp.float32),
            pltpu.VMEM((NZ * 16, wide), bf16),
            dma((PLACES + 1,)), dma((2, PLACES)), dma,
        ],
        compiler_params=pltpu.CompilerParams(vmem_limit_bytes=32 * 1024 * 1024),
        cost_estimate=pl.CostEstimate(flops=0, bytes_accessed=4 * 2**20, transcendentals=0),
    )(result)
    return attended, lse.T, grad


def solution(mesh):
    in_specs = (
        P(("dp", "ctx"), None),
        P(("dp", "ctx"), None),
        P(("dp", "ctx"), None),
        P(("dp", "ctx"), None),
        P("dp", None),
        P("dp", "ctx", None, None),
    )
    out_specs = (P(("dp", "ctx"), None), P(("dp", "ctx"), None), P(("dp", "ctx"), None))
    return jax.shard_map(local, mesh=mesh, in_specs=in_specs, out_specs=out_specs, check_vma=False)
```

time: 99.1 us -> 88.8 us (0.90)
  Pallas kernels: 91.1 us -> 82.3 us
  local copies, waits for them, and re-layouts: 6.95 us -> 5.61 us
    pallas_call x2, Pallas kernels: 91.1 us -> 82.3 us  [the longest x1 80.4 us: local(): pl.pallas_call(kernel, out_shape=jax.ShapeDtypeStruct((KV_HEADS, NY, TILE...]
    unnamed x14 -> x12, local copies, waits for them, and re-layouts: 6.95 us -> 5.61 us
where the time goes in v3:
time: 88.8 us; the launch traced here: 88.6 us
  Pallas kernels  82.3 us (93%)
  local copies, waits for them, and re-layouts  5.61 us (6%)
    pallas_call x1, Pallas kernels, local(): pl.pallas_call(kernel, out_shape=jax.ShapeDtypeStruct((KV_HEADS, NY, TILE...  80.4 us
    unnamed x12, local copies, waits for them, and re-layouts  5.61 us
    pallas_call x1, Pallas kernels, local(): pl.pallas_call(order_results, out_shape=(jax.ShapeDtypeStruct((NZ * 16, w...  1.9 us

profile of v3, /device:TPU:1, one launch (start us, length us, event | category | flops | bytes accessed | tf_op | source)
XLA Modules:
  0.0 88.6 jit_solution(4540682246422367828)
XLA Ops:
  0.6 0.0 copy-start
  0.6 1.2 %copy-done = bf16[128,4096]{1,0:T(8,128)(2,1)S(1)} copy-done((bf16[128,4096]{1,0:T(8,128)(2,1)S(1)}, bf16[128,4096]{1,0:T(8,128)(2,1)}, u32[]{:S(2)}) %copy-start) | copy-done | bytes 1048600
  1.9 0.0 copy-start.1
  1.9 1.2 %copy-done.1 = bf16[128,4096]{1,0:T(8,128)(2,1)S(1)} copy-done((bf16[128,4096]{1,0:T(8,128)(2,1)S(1)}, bf16[128,4096]{1,0:T(8,128)(2,1)}, u32[]{:S(2)}) %copy-start.1) | copy-done | bytes 1048600
  3.1 0.0 copy-start.2
  3.1 0.9 %copy-done.2 = bf16[128,512]{1,0:T(8,128)(2,1)S(1)} copy-done((bf16[128,512]{1,0:T(8,128)(2,1)S(1)}, bf16[128,512]{1,0:T(8,128)(2,1)}, u32[]{:S(2)}) %copy-start.2) | copy-done | bytes 131096
  4.0 0.0 copy-start.3
  4.0 0.9 %copy-done.3 = bf16[128,512]{1,0:T(8,128)(2,1)S(1)} copy-done((bf16[128,512]{1,0:T(8,128)(2,1)S(1)}, bf16[128,512]{1,0:T(8,128)(2,1)}, u32[]{:S(2)}) %copy-start.3) | copy-done | bytes 131096
  4.9 0.0 copy-start.4
  4.9 0.7 copy-done.4
  5.6 0.0 copy-start.5
  5.6 0.7 copy-done.5
  6.3 80.4 %shard_map.85.got = bf16[4,8,33,8,128]{4,3,2,1,0:T(8,128)(2,1)S(1)} custom-call(bf16[128,4096]{1,0:T(8,128)(2,1)S(1)} %copy-done, bf16[128,4096]{1,0:T(8,128)(2,1)S(1)} %copy-done.1, bf16[128,512]{1,0:T(8,128)(2,1)S(1)} %copy-done.2, bf16[128,512]{1,0:T(8,128)(2,1)S(1)} %copy-done.3, s32[2,8]{1,0:T(2,128)S(1)} %copy-done.4, s32[2,64]{1,0:T(2,128)S(1)} %bitcast.4), custom_call_target="tpu_custom_call" | custom-call | flops 4000000000 | bytes 8388608 | tf_op jit(solution)/shard_map/pallas_call | solution.py:380
  86.7 1.9 %shard_map.86 = (bf16[128,4096]{1,0:T(8,128)(2,1)}, f32[32,128]{1,0:T(8,128)}, bf16[128,4096]{1,0:T(8,128)(2,1)}) custom-call(bf16[4,8,33,8,128]{4,3,2,1,0:T(8,128)(2,1)S(1)} %shard_map.85.got), custom_call_target="tpu_custom_call" | custom-call | bytes 4194304 | tf_op jit(solution)/shard_map/pallas_call | solution.py:410
Async XLA Ops:
  0.6 1.2 %copy-start = (bf16[128,4096]{1,0:T(8,128)(2,1)S(1)}, bf16[128,4096]{1,0:T(8,128)(2,1)}, u32[]{:S(2)}) copy-start(bf16[128,4096]{1,0:T(8,128)(2,1)} %queries.1) | copy-start | bytes 3145732
  1.9 1.2 %copy-start.1 = (bf16[128,4096]{1,0:T(8,128)(2,1)S(1)}, bf16[128,4096]{1,0:T(8,128)(2,1)}, u32[]{:S(2)}) copy-start(bf16[128,4096]{1,0:T(8,128)(2,1)} %grads.1) | copy-start | bytes 3145732
  3.1 0.9 %copy-start.2 = (bf16[128,512]{1,0:T(8,128)(2,1)S(1)}, bf16[128,512]{1,0:T(8,128)(2,1)}, u32[]{:S(2)}) copy-start(bf16[128,512]{1,0:T(8,128)(2,1)} %keys.1) | copy-start | bytes 393220
  4.0 0.9 %copy-start.3 = (bf16[128,512]{1,0:T(8,128)(2,1)S(1)}, bf16[128,512]{1,0:T(8,128)(2,1)}, u32[]{:S(2)}) copy-start(bf16[128,512]{1,0:T(8,128)(2,1)} %values.1) | copy-start | bytes 393220
  4.9 0.7 copy-start.4
  5.6 0.7 copy-start.5

commit v4 on v3

--- a/solution.py
+++ b/solution.py
@@ -24,8 +24,9 @@
 TILES = 4 * PLACES + 1
 EARLY = 3
 STEPS = (0, 1, 3, 2)
-KV_ROWS = 272
+KV_ROWS = 256
 NEG_FILL = -1e30
+VMEM_BYTES = 63 * 1024 * 1024
 MESH = pl.DeviceIdType.MESH
 
 
@@ -39,9 +40,9 @@
 
 def kernel(queries, grads, keys, values, lengths, positions, out,
            query_in, grad_in, key_in, value_in, lengths_in, positions_in,
-           rows, kv_out, kv, got, res, lse, second,
+           rows, kv_out, marks_out, marks_in, marks, bounds, kv, got, res, lse, second,
            load, small_load, row_send, row_recv, kva_send, kvb_send, kv_recv, ring_send, ring_recv,
-           res_send, res_recv):
+           marka_send, markb_send, mark_recv, marks_send, marks_recv, res_send, res_recv):
     dp = lax.axis_index("dp")
     ctx = lax.axis_index("ctx")
     z, y = lax.div(dp, NY), lax.rem(dp, NY)
@@ -55,11 +56,23 @@
     def at_ctx(x_step, core_step):
         return lax.rem(x + x_step, NX) * 2 + lax.rem(core + core_step, 2)
 
+    def load_small(i):
+        source, target = ((keys, key_in), (values, value_in), (lengths, lengths_in),
+                          (positions, positions_in))[i]
+        return pltpu.make_async_copy(source, target, small_load.at[i])
+
+    for i in range(4):
+        load_small(i).start()
+
     barrier = pltpu.get_barrier_semaphore()
-    line = [(z * NY + at_y(step), ctx) for step in (1, -1, 2, -2, 4)]
+    line = [(z * NY + at_y(step), ctx) for step in (1, -1, 2, -2)]
     near = [(dp, at_ctx(x_step, core_step)) for x_step in range(NX) for core_step in range(2)
             if x_step or core_step]
-    for dev in line + near + [(left, ctx), (right, ctx)]:
+    far = z * NY + at_y(4)
+    opposite = [(far, at_ctx(x_step, core_step)) for x_step in range(NX) for core_step in range(2)]
+    ring_line = [(lax.rem(z + step, NZ) * NY + y, ctx) for step in range(1, NZ)]
+    first_round = near + opposite + line + ring_line
+    for dev in first_round:
         pl.semaphore_signal(barrier, inc=1, device_id=dev, device_id_type=MESH)
 
     def load_rows(home_z, which):
@@ -67,16 +80,9 @@
         source, target = ((queries, query_in), (grads, grad_in))[which]
         return pltpu.make_async_copy(source.at[block], target.at[block], load.at[which, home_z])
 
-    small = [pltpu.make_async_copy(source, target, small_load.at[i])
-             for i, (source, target) in enumerate(((lengths, lengths_in), (positions, positions_in),
-                                                   (keys, key_in), (values, value_in)))]
-    for copy in small:
-        copy.start()
     for home_z in range(NZ):
         for which in range(2):
             load_rows(home_z, which).start()
-    for copy in small:
-        copy.wait()
 
     def order_rows(home_z, carry):
         place = rank(lax.rem(home_z - z + NZ, NZ))
@@ -90,6 +96,43 @@
                     rows[head * NY + home_y, place, which] = block[2 * home_y:2 * home_y + 2]
         return carry
 
+    def remote(src, dst, send, recv, dev):
+        return pltpu.make_async_remote_copy(src_ref=src, dst_ref=dst, send_sem=send, recv_sem=recv,
+                                            device_id=dev, device_id_type=MESH)
+
+    def wait_bytes(ref, sem):
+        pltpu.make_async_copy(ref, ref, sem).wait()
+
+    load_small(0).wait()
+    load_small(1).wait()
+    for head in range(KV_HEADS):
+        cols = slice(head * HEAD_DIM, (head + 1) * HEAD_DIM)
+        kv_out[head, 0:128] = key_in[:, cols]
+        kv_out[head, 128:256] = value_in[:, cols]
+
+    pl.semaphore_wait(barrier, len(first_round))
+    for dev in line:
+        pl.semaphore_signal(second, inc=1, device_id=dev, device_id_type=MESH)
+
+    here = kv.at[z, ctx]
+    arrived = kv_recv.at[x]
+
+    @pl.when(core == 0)
+    def _():
+        pltpu.make_async_copy(kv_out.at[x], here, arrived).start()
+
+    @pl.when(core != 0)
+    def _():
+        remote(kv_out.at[x], here, kva_send, arrived, (dp, x * 2)).start()
+
+    remote(kv_out.at[x], here, kvb_send, arrived, (far, x * 2 + 1)).start()
+    for x_step in STEPS[1:]:
+        head = lax.rem(x + x_step, NX)
+        remote(kv_out.at[head], here, kva_send, arrived, (dp, head * 2)).start()
+        remote(kv_out.at[head], here, kvb_send, arrived, (far, head * 2 + 1)).start()
+
+    load_small(2).wait()
+    load_small(3).wait()
     pos = positions_in[...]
     spans = lengths_in[...]
     doc_lane = lax.broadcasted_iota(jnp.int32, (SUBS, 8), 1)
@@ -112,52 +155,31 @@
     wanted = lax.rem(lax.div(lane8, 32), 2) * 4 + lax.rem(lane8, 4)
 
     for copy in range(2):
-        marks = []
+        made = []
         for e_hi in range(2):
             low, high = [at_y(4 * copy + y_step(2 * e_hi + e_lo, core)) for e_lo in range(2)]
             source = jnp.where(lane64 < 64, low, high) + lax.rem(lax.div(lane64, 4), NZ) * NY
             pick_rows = (row64 == source).astype(jnp.float32).astype(jnp.bfloat16)
             found = jnp.dot(table, pick_rows, preferred_element_type=jnp.float32)
             found = jnp.sum(jnp.where(row8 == wanted, found, 0.0), axis=0, keepdims=True)
-            marks.append(jnp.broadcast_to(found, (GROUP, 128)))
-        marks = jnp.concatenate(marks, axis=0).astype(jnp.bfloat16)
-        for head in range(KV_HEADS):
-            cols = slice(head * HEAD_DIM, (head + 1) * HEAD_DIM)
-            kv_out[copy, head, 0:128] = key_in[:, cols]
-            kv_out[copy, head, 128:256] = value_in[:, cols]
-            kv_out[copy, head, 256:272] = marks
-
-    lax.fori_loop(0, NZ, order_rows, 0)
-
-    pl.semaphore_wait(barrier, len(line) + len(near) + 2)
-    for dev in line:
-        pl.semaphore_signal(second, inc=1, device_id=dev, device_id_type=MESH)
-    pl.semaphore_wait(second, len(line))
-
-    def remote(src, dst, send, recv, dev):
-        return pltpu.make_async_remote_copy(src_ref=src, dst_ref=dst, send_sem=send, recv_sem=recv,
-                                            device_id=dev, device_id_type=MESH)
-
-    def wait_bytes(ref, sem):
-        pltpu.make_async_copy(ref, ref, sem).wait()
-
-    here = kv.at[z, ctx]
-    arrived = kv_recv.at[x]
+            made.append(jnp.broadcast_to(found, (GROUP, 128)))
+        made = jnp.concatenate(made, axis=0).astype(jnp.bfloat16)
+        marks_out[copy] = made
+    marks_here = marks_in.at[ctx]
 
     @pl.when(core == 0)
     def _():
-        pltpu.make_async_copy(kv_out.at[0, x], here, arrived).start()
+        pltpu.make_async_copy(marks_out.at[0], marks_here, mark_recv).start()
 
     @pl.when(core != 0)
     def _():
-        remote(kv_out.at[0, x], here, kva_send, arrived, (dp, x * 2)).start()
-
-    far = z * NY + at_y(4)
-    remote(kv_out.at[1, x], here, kvb_send, arrived, (far, x * 2 + 1)).start()
+        remote(marks_out.at[0], marks_here, marka_send, mark_recv, (dp, x * 2)).start()
+
+    remote(marks_out.at[1], marks_here, markb_send, mark_recv, (far, x * 2 + 1)).start()
     for x_step in STEPS[1:]:
         head = lax.rem(x + x_step, NX)
-        remote(kv_out.at[0, head], here, kva_send, arrived, (dp, head * 2)).start()
-        remote(kv_out.at[1, head], here, kvb_send, arrived, (far, head * 2 + 1)).start()
+        remote(marks_out.at[0], marks_here, marka_send, mark_recv, (dp, head * 2)).start()
+        remote(marks_out.at[1], marks_here, markb_send, mark_recv, (far, head * 2 + 1)).start()
 
     def send_rows(part, which_e):
         ranks = pl.ds(0, EARLY) if part == 0 else pl.ds(EARLY, PLACES - EARLY)
@@ -209,15 +231,24 @@
             if step < 3:
                 forward(step + 1, i)
 
-    send_rows(0, (0, 2, 3, 1))
     begin_ring(0)
-    send_rows(1, (0,))
+    lax.fori_loop(0, NZ, order_rows, 0)
+    pl.semaphore_wait(second, len(line))
     begin_ring(1)
-    send_rows(1, (2,))
+    send_rows(0, (0, 2))
     begin_ring(2)
-    send_rows(1, (3,))
+    send_rows(0, (3, 1))
     begin_ring(3)
-    send_rows(1, (1,))
+    send_rows(1, (0, 2, 3, 1))
+
+    row16 = lax.broadcasted_iota(jnp.int32, (16, 128), 0)
+    col16 = lax.broadcasted_iota(jnp.int32, (16, 128), 1)
+    wait_bytes(marks_in, mark_recv)
+    thin = (col16 == row16 * GROUP).astype(jnp.float32).astype(jnp.bfloat16)
+    marks[z] = jnp.dot(thin, marks_in[...].reshape(128, 128),
+                       preferred_element_type=jnp.float32).astype(jnp.bfloat16)
+    for dev in ring_line:
+        remote(marks.at[z], marks.at[z], marks_send, marks_recv, dev).start()
 
     scale = 1.0 / math.sqrt(HEAD_DIM)
     to_log2 = scale * math.log2(math.e)
@@ -232,19 +263,28 @@
     def dot(a, b, dims):
         return lax.dot_general(a, b, (dims, ((), ())), preferred_element_type=jnp.float32)
 
+    row128 = lax.broadcasted_iota(jnp.int32, (128, 16), 0)
+    col128 = lax.broadcasted_iota(jnp.int32, (128, 16), 1)
+    widen = (lax.div(row128, GROUP) == col128).astype(jnp.float32).astype(jnp.bfloat16)
+
+    def make_bounds(chunk, carry):
+        wide = jnp.dot(widen, marks[chunk], preferred_element_type=jnp.float32).astype(jnp.bfloat16)
+        for s in range(SUBS):
+            for which in range(2):
+                for e_lo in range(2):
+                    base = e_lo * 64 + s * 32 + z * 4 + which * 2
+                    bounds[chunk * SUBS + s, which, e_lo * 128:(e_lo + 1) * 128] = dot(
+                        wide, pick(base), ((1,), (0,)))
+        return carry
+
     def one_sequence(n, chunk, s):
         q = got[:, n, 0, s].reshape(256, HEAD_DIM)
         g = got[:, n, 1, s].reshape(256, HEAD_DIM)
         k = kv[chunk, :, pl.ds(pl.multiple_of(s * HALF, HALF), HALF), :].reshape(SEQ, HEAD_DIM)
         v = kv[chunk, :, pl.ds(pl.multiple_of(128 + s * HALF, HALF), HALF), :].reshape(SEQ, HEAD_DIM)
-        marks = kv[chunk, :, pl.ds(256, 16), :].reshape(128, 128)
-        bounds = []
-        for which in range(2):
-            halves = [dot(marks, pick(e_lo * 64 + s * 32 + z * 4 + which * 2), ((1,), (0,)))
-                      for e_lo in range(2)]
-            whole = jnp.concatenate(halves, axis=0)
-            bounds.append(jnp.concatenate([whole] * 4, axis=1))
-        visible = jnp.logical_and(key_pos <= bounds[0], key_pos >= bounds[1])
+        last, first = [jnp.concatenate([bounds[chunk * SUBS + s, which]] * 4, axis=1)
+                       for which in range(2)]
+        visible = jnp.logical_and(key_pos <= last, key_pos >= first)
         scores = jnp.where(visible, dot(q, k, ((1,), (1,))) * to_log2, NEG_FILL)
         top = jnp.max(scores, axis=1, keepdims=True)
         p = jnp.exp2(scores - top)
@@ -272,10 +312,11 @@
             one_sequence(n, chunk, s)
             return inner
 
-        return lax.fori_loop(0, SUBS, sub, carry)
-
-    def give(lower, upper):
-        tiles = pl.ds(lower * 4, (upper - lower) * 4 + (1 if upper == PLACES else 0))
+        lax.fori_loop(0, SUBS, sub, 0)
+        give(pl.ds(n * 4, 4))
+        return carry
+
+    def give(tiles):
         dst = out.at[x, server_home, tiles]
         for e in (0, 2, 3, 1):
             for other in range(2):
@@ -290,34 +331,37 @@
                         remote(src, dst, res_send, res_recv, (z * NY + home_y, home_ctx)).start()
 
     lse[...] = jnp.zeros_like(lse)
+    wait_bytes(marks.at[pl.ds(0, NZ - 1)], marks_recv)
+    lax.fori_loop(0, NZ, make_bounds, 0)
     pass_on(0)
     wait_bytes(got.at[:, pl.ds(0, EARLY)], row_recv.at[0])
     lax.fori_loop(0, 3, serve, 0)
-    give(0, 3)
     pass_on(1)
     wait_bytes(got.at[:, pl.ds(EARLY, PLACES - EARLY)], row_recv.at[1])
     lax.fori_loop(3, 5, serve, 0)
-    give(3, 5)
     pass_on(2)
     lax.fori_loop(5, 7, serve, 0)
-    give(5, 7)
     pass_on(3)
     lax.fori_loop(7, 8, serve, 0)
     res[:, 4 * PLACES] = lse[...].astype(jnp.bfloat16).reshape(SLOTS, GROUP, 128)
-    give(7, 8)
+    give(pl.ds(4 * PLACES, 1))
 
     sent = pl.ds(0, SLOTS - 1)
     wait_bytes(rows.at[sent, pl.ds(0, EARLY)], row_send.at[0])
     wait_bytes(rows.at[sent, pl.ds(EARLY, PLACES - EARLY)], row_send.at[1])
     wait_bytes(kv.at[0, pl.ds(0, 4)], kvb_send)
+    wait_bytes(marks_in.at[pl.ds(0, 4)], markb_send)
+    wait_bytes(marks.at[pl.ds(0, NZ - 1)], marks_send)
 
     @pl.when(core == 0)
     def _():
         wait_bytes(kv.at[0, pl.ds(0, 3)], kva_send)
+        wait_bytes(marks_in.at[pl.ds(0, 3)], marka_send)
 
     @pl.when(core != 0)
     def _():
         wait_bytes(kv.at[0, pl.ds(0, 4)], kva_send)
+        wait_bytes(marks_in.at[pl.ds(0, 4)], marka_send)
 
     for step in range(4):
         for way in range(2):
@@ -390,17 +434,21 @@
             pltpu.VMEM((SUBS, 8), jnp.int32),
             pltpu.VMEM((SUBS, HALF), jnp.int32),
             pltpu.VMEM((SLOTS, PLACES, 2, SUBS, GROUP, HEAD_DIM), bf16),
-            pltpu.VMEM((2, KV_HEADS, KV_ROWS, HEAD_DIM), bf16),
+            pltpu.VMEM((KV_HEADS, KV_ROWS, HEAD_DIM), bf16),
+            pltpu.VMEM((2, 16, 128), bf16),
+            pltpu.VMEM((NCTX, 16, 128), bf16),
+            pltpu.VMEM((NZ, 16, 128), bf16),
+            pltpu.VMEM((NZ * SUBS, 2, SLOTS * GROUP, 128), jnp.float32),
             pltpu.VMEM((NZ, NCTX, KV_ROWS, HEAD_DIM), bf16),
             pltpu.VMEM((SLOTS, PLACES, 2, SUBS, GROUP, HEAD_DIM), bf16),
             pltpu.VMEM((SLOTS, TILES, GROUP, HEAD_DIM), bf16),
             pltpu.VMEM((SLOTS * GROUP, 128), jnp.float32),
             pltpu.SemaphoreType.REGULAR,
             dma((2, NZ)), dma((4,)), dma((2,)), dma((2,)), dma, dma, dma((NX,)),
-            dma((2, 4)), dma((2, 4, NX)), dma, dma,
+            dma((2, 4)), dma((2, 4, NX)), dma, dma, dma, dma, dma, dma, dma,
         ],
         compiler_params=pltpu.CompilerParams(
-            collective_id=0, has_side_effects=True, vmem_limit_bytes=48 * 1024 * 1024
+            collective_id=0, has_side_effects=True, vmem_limit_bytes=VMEM_BYTES
         ),
         cost_estimate=pl.CostEstimate(flops=4 * 10**9, bytes_accessed=8 * 2**20,
                                       transcendentals=2 * 2**20),
@@ -423,7 +471,7 @@
             pltpu.VMEM((NZ * 16, wide), bf16),
             dma((PLACES + 1,)), dma((2, PLACES)), dma,
         ],
-        compiler_params=pltpu.CompilerParams(vmem_limit_bytes=32 * 1024 * 1024),
+        compiler_params=pltpu.CompilerParams(vmem_limit_bytes=VMEM_BYTES),
         cost_estimate=pl.CostEstimate(flops=0, bytes_accessed=4 * 2**20, transcendentals=0),
     )(result)
     return attended, lse.T, grad

time: 88.8 us -> 82.2 us (0.926)
  local copies, waits for them, and re-layouts: 5.61 us -> 0 us
  Pallas kernels: 82.3 us -> 80.6 us
    unnamed x12 -> x0, local copies, waits for them, and re-layouts: 5.61 us -> none
    pallas_call x1, Pallas kernels: 80.4 us -> 78 us  [local(): pl.pallas_call(kernel, out_shape=jax.ShapeDtypeStruct((KV_HEADS, NY, TILE...]
where the time goes in v4:
time: 82.2 us; the launch traced here: 81.3 us
  Pallas kernels  80.6 us (98%)
    pallas_call x1, Pallas kernels, local(): pl.pallas_call(kernel, out_shape=jax.ShapeDtypeStruct((KV_HEADS, NY, TILE...  78 us
    pallas_call x1, Pallas kernels, local(): pl.pallas_call(order_results, out_shape=(jax.ShapeDtypeStruct((NZ * 16, w...  2.58 us

profile of v4, /device:TPU:1, one launch (start us, length us, event | category | flops | bytes accessed | tf_op | source)
XLA Modules:
  0.0 81.3 jit_solution(2274963509307684540)
XLA Ops:
  0.6 78.0 %shard_map.85.got = bf16[4,8,33,8,128]{4,3,2,1,0:T(8,128)(2,1)} custom-call(bf16[128,4096]{1,0:T(8,128)(2,1)} %queries.1, bf16[128,4096]{1,0:T(8,128)(2,1)} %grads.1, bf16[128,512]{1,0:T(8,128)(2,1)} %keys.1, bf16[128,512]{1,0:T(8,128)(2,1)} %values.1, s32[2,8]{1,0:T(2,128)} %lengths.1, s32[2,64]{1,0:T(2,128)} %bitcast.5), custom_call_target="tpu_custom_call" | custom-call | flops 4000000000 | bytes 8388608 | tf_op jit(solution)/shard_map/pallas_call | solution.py:424
  78.7 2.6 %shard_map.86 = (bf16[128,4096]{1,0:T(8,128)(2,1)}, f32[32,128]{1,0:T(8,128)}, bf16[128,4096]{1,0:T(8,128)(2,1)}) custom-call(bf16[4,8,33,8,128]{4,3,2,1,0:T(8,128)(2,1)} %shard_map.85.got), custom_call_target="tpu_custom_call" | custom-call | bytes 4194304 | tf_op jit(solution)/shard_map/pallas_call | solution.py:458

commit v5 on v4

--- a/solution.py
+++ b/solution.py
@@ -222,8 +222,8 @@
         wait_bytes(piece(z, i), kv_recv.at[lax.rem(x + STEPS[i], NX)])
         forward(0, i)
 
-    def pass_on(step):
-        for i in range(NX):
+    def pass_on(step, which=range(NX)):
+        for i in which:
             if i in pieces(step, 0):
                 wait_bytes(piece(from_left(step + 1), i), ring_recv.at[0, step, i])
             if i in pieces(step, 1):
@@ -231,15 +231,17 @@
             if step < 3:
                 forward(step + 1, i)
 
-    begin_ring(0)
+    def begin_on(which_core, which):
+        @pl.when(core == which_core)
+        def _():
+            for i in which:
+                begin_ring(i)
+
+    begin_on(0, range(NX))
     lax.fori_loop(0, NZ, order_rows, 0)
     pl.semaphore_wait(second, len(line))
-    begin_ring(1)
-    send_rows(0, (0, 2))
-    begin_ring(2)
-    send_rows(0, (3, 1))
-    begin_ring(3)
-    send_rows(1, (0, 2, 3, 1))
+    begin_on(1, (0,))
+    send_rows(0, (0, 2, 3, 1))
 
     row16 = lax.broadcasted_iota(jnp.int32, (16, 128), 0)
     col16 = lax.broadcasted_iota(jnp.int32, (16, 128), 1)
@@ -249,6 +251,10 @@
                        preferred_element_type=jnp.float32).astype(jnp.bfloat16)
     for dev in ring_line:
         remote(marks.at[z], marks.at[z], marks_send, marks_recv, dev).start()
+    begin_on(1, (1, 2))
+    send_rows(1, (0, 2))
+    begin_on(1, (3,))
+    send_rows(1, (3, 1))
 
     scale = 1.0 / math.sqrt(HEAD_DIM)
     to_log2 = scale * math.log2(math.e)
@@ -305,17 +311,6 @@
             kept = jnp.where(lse_lane == part * 16 + chunk * SUBS + s, term, kept)
         lse[...] = kept
 
-    def serve(n, carry):
-        chunk = lax.rem(z + lax.div(n + 1, 2) * (2 * lax.rem(n, 2) - 1) + NZ, NZ)
-
-        def sub(s, inner):
-            one_sequence(n, chunk, s)
-            return inner
-
-        lax.fori_loop(0, SUBS, sub, 0)
-        give(pl.ds(n * 4, 4))
-        return carry
-
     def give(tiles):
         dst = out.at[x, server_home, tiles]
         for e in (0, 2, 3, 1):
@@ -330,19 +325,45 @@
                     else:
                         remote(src, dst, res_send, res_recv, (z * NY + home_y, home_ctx)).start()
 
+    def rest_of_rows():
+        wait_bytes(got.at[:, pl.ds(EARLY, PLACES - EARLY)], row_recv.at[1])
+
+    def before(n):
+        if n == 0:
+            wait_bytes(got.at[:, pl.ds(0, EARLY)], row_recv.at[0])
+        elif n == 1:
+            pass_on(1, (0,))
+        elif n == 2:
+            pass_on(1, (1,))
+        elif n == 3:
+            pass_on(1, (2, 3))
+            pass_on(2, (0,))
+            rest_of_rows()
+        elif n == 4:
+            pass_on(2, (1,))
+        elif n == 5:
+            pass_on(2, (2, 3))
+        elif n == 7:
+            pass_on(3)
+
+    def serve(n, carry):
+        for turn in (0, 1, 2, 3, 4, 5, 7):
+            pl.when(n == turn)(functools.partial(before, turn))
+        chunk = lax.rem(z + lax.div(n + 1, 2) * (2 * lax.rem(n, 2) - 1) + NZ, NZ)
+
+        def sub(s, inner):
+            one_sequence(n, chunk, s)
+            return inner
+
+        lax.fori_loop(0, SUBS, sub, 0)
+        give(pl.ds(n * 4, 4))
+        return carry
+
     lse[...] = jnp.zeros_like(lse)
+    pass_on(0)
     wait_bytes(marks.at[pl.ds(0, NZ - 1)], marks_recv)
     lax.fori_loop(0, NZ, make_bounds, 0)
-    pass_on(0)
-    wait_bytes(got.at[:, pl.ds(0, EARLY)], row_recv.at[0])
-    lax.fori_loop(0, 3, serve, 0)
-    pass_on(1)
-    wait_bytes(got.at[:, pl.ds(EARLY, PLACES - EARLY)], row_recv.at[1])
-    lax.fori_loop(3, 5, serve, 0)
-    pass_on(2)
-    lax.fori_loop(5, 7, serve, 0)
-    pass_on(3)
-    lax.fori_loop(7, 8, serve, 0)
+    lax.fori_loop(0, PLACES, serve, 0)
     res[:, 4 * PLACES] = lse[...].astype(jnp.bfloat16).reshape(SLOTS, GROUP, 128)
     give(pl.ds(4 * PLACES, 1))
 

time: 82.2 us -> 79.7 us (0.970)
  Pallas kernels: 80.6 us -> 78.9 us
    pallas_call x1, Pallas kernels: 78 us -> 76.3 us  [local(): pl.pallas_call(kernel, out_shape=jax.ShapeDtypeStruct((KV_HEADS, NY, TILE...]
where the time goes in v5:
time: 79.7 us; the launch traced here: 79.5 us
  Pallas kernels  78.9 us (99%)
    pallas_call x1, Pallas kernels, local(): pl.pallas_call(kernel, out_shape=jax.ShapeDtypeStruct((KV_HEADS, NY, TILE...  76.3 us
    pallas_call x1, Pallas kernels, local(): pl.pallas_call(order_results, out_shape=(jax.ShapeDtypeStruct((NZ * 16, w...  2.57 us

profile of v5, /device:TPU:1, one launch (start us, length us, event | category | flops | bytes accessed | tf_op | source)
XLA Modules:
  0.0 79.5 jit_solution(4749765385454516129)
XLA Ops:
  0.6 76.3 %shard_map.85.got = bf16[4,8,33,8,128]{4,3,2,1,0:T(8,128)(2,1)} custom-call(bf16[128,4096]{1,0:T(8,128)(2,1)} %queries.1, bf16[128,4096]{1,0:T(8,128)(2,1)} %grads.1, bf16[128,512]{1,0:T(8,128)(2,1)} %keys.1, bf16[128,512]{1,0:T(8,128)(2,1)} %values.1, s32[2,8]{1,0:T(2,128)} %lengths.1, s32[2,64]{1,0:T(2,128)} %bitcast.5), custom_call_target="tpu_custom_call" | custom-call | flops 4000000000 | bytes 8388608 | tf_op jit(solution)/shard_map/pallas_call | solution.py:445
  76.9 2.6 %shard_map.86 = (bf16[128,4096]{1,0:T(8,128)(2,1)}, f32[32,128]{1,0:T(8,128)}, bf16[128,4096]{1,0:T(8,128)(2,1)}) custom-call(bf16[4,8,33,8,128]{4,3,2,1,0:T(8,128)(2,1)} %shard_map.85.got), custom_call_target="tpu_custom_call" | custom-call | bytes 4194304 | tf_op jit(solution)/shard_map/pallas_call | solution.py:479

commit v6 on v5

--- a/solution.py
+++ b/solution.py
@@ -21,7 +21,7 @@
 HALF = 64
 SEQ = 512
 PLACES = NY
-TILES = 4 * PLACES + 1
+TILES = 4 * PLACES + SUBS
 EARLY = 3
 STEPS = (0, 1, 3, 2)
 KV_ROWS = 256
@@ -30,8 +30,12 @@
 MESH = pl.DeviceIdType.MESH
 
 
-def y_step(e, core):
-    return e - 1 - 4 * core * (e // 3)
+def y_step(e, copy, s):
+    return e - 1 - 4 * (e // 3) * (copy if s else 1 - copy)
+
+
+def away(copy, s):
+    return (3 - 6 * s) * copy
 
 
 def rank(distance):
@@ -68,8 +72,9 @@
     line = [(z * NY + at_y(step), ctx) for step in (1, -1, 2, -2)]
     near = [(dp, at_ctx(x_step, core_step)) for x_step in range(NX) for core_step in range(2)
             if x_step or core_step]
-    far = z * NY + at_y(4)
-    opposite = [(far, at_ctx(x_step, core_step)) for x_step in range(NX) for core_step in range(2)]
+    far = [z * NY + at_y(away(1, s)) for s in range(SUBS)]
+    opposite = [(dev, at_ctx(x_step, core_step)) for dev in far for x_step in range(NX)
+                for core_step in range(2)]
     ring_line = [(lax.rem(z + step, NZ) * NY + y, ctx) for step in range(1, NZ)]
     first_round = near + opposite + line + ring_line
     for dev in first_round:
@@ -93,7 +98,8 @@
                 block = source[lines, head * GROUP * HEAD_DIM:(head + 1) * GROUP * HEAD_DIM]
                 block = block.reshape(16, GROUP, HEAD_DIM)
                 for home_y in range(NY):
-                    rows[head * NY + home_y, place, which] = block[2 * home_y:2 * home_y + 2]
+                    for s in range(SUBS):
+                        rows[head * NY + home_y, s, place, which] = block[2 * home_y + s]
         return carry
 
     def remote(src, dst, send, recv, dev):
@@ -107,8 +113,9 @@
     load_small(1).wait()
     for head in range(KV_HEADS):
         cols = slice(head * HEAD_DIM, (head + 1) * HEAD_DIM)
-        kv_out[head, 0:128] = key_in[:, cols]
-        kv_out[head, 128:256] = value_in[:, cols]
+        for s in range(SUBS):
+            kv_out[head, s * 128:s * 128 + HALF] = key_in[s * HALF:(s + 1) * HALF, cols]
+            kv_out[head, s * 128 + HALF:(s + 1) * 128] = value_in[s * HALF:(s + 1) * HALF, cols]
 
     pl.semaphore_wait(barrier, len(first_round))
     for dev in line:
@@ -125,11 +132,17 @@
     def _():
         remote(kv_out.at[x], here, kva_send, arrived, (dp, x * 2)).start()
 
-    remote(kv_out.at[x], here, kvb_send, arrived, (far, x * 2 + 1)).start()
+    def send_far(head):
+        for s in range(SUBS):
+            lines = pl.ds(s * 128, 128)
+            remote(kv_out.at[head, lines], here.at[lines], kvb_send, arrived,
+                   (far[s], head * 2 + 1)).start()
+
+    send_far(x)
     for x_step in STEPS[1:]:
         head = lax.rem(x + x_step, NX)
         remote(kv_out.at[head], here, kva_send, arrived, (dp, head * 2)).start()
-        remote(kv_out.at[head], here, kvb_send, arrived, (far, head * 2 + 1)).start()
+        send_far(head)
 
     load_small(2).wait()
     load_small(3).wait()
@@ -157,7 +170,10 @@
     for copy in range(2):
         made = []
         for e_hi in range(2):
-            low, high = [at_y(4 * copy + y_step(2 * e_hi + e_lo, core)) for e_lo in range(2)]
+            low, high = [
+                jnp.where(lax.rem(lax.div(lane64, 32), 2) == 0,
+                          *[at_y(away(copy, s) + y_step(2 * e_hi + e_lo, copy, s)) for s in range(SUBS)])
+                for e_lo in range(2)]
             source = jnp.where(lane64 < 64, low, high) + lax.rem(lax.div(lane64, 4), NZ) * NY
             pick_rows = (row64 == source).astype(jnp.float32).astype(jnp.bfloat16)
             found = jnp.dot(table, pick_rows, preferred_element_type=jnp.float32)
@@ -165,38 +181,42 @@
             made.append(jnp.broadcast_to(found, (GROUP, 128)))
         made = jnp.concatenate(made, axis=0).astype(jnp.bfloat16)
         marks_out[copy] = made
-    marks_here = marks_in.at[ctx]
 
     @pl.when(core == 0)
     def _():
-        pltpu.make_async_copy(marks_out.at[0], marks_here, mark_recv).start()
+        for s in range(SUBS):
+            pltpu.make_async_copy(marks_out.at[0], marks_in.at[s, ctx], mark_recv).start()
 
     @pl.when(core != 0)
     def _():
-        remote(marks_out.at[0], marks_here, marka_send, mark_recv, (dp, x * 2)).start()
-
-    remote(marks_out.at[1], marks_here, markb_send, mark_recv, (far, x * 2 + 1)).start()
-    for x_step in STEPS[1:]:
+        for s in range(SUBS):
+            remote(marks_out.at[0], marks_in.at[s, ctx], marka_send, mark_recv, (dp, x * 2)).start()
+
+    for x_step in STEPS:
         head = lax.rem(x + x_step, NX)
-        remote(marks_out.at[0], marks_here, marka_send, mark_recv, (dp, head * 2)).start()
-        remote(marks_out.at[1], marks_here, markb_send, mark_recv, (far, head * 2 + 1)).start()
+        for s in range(SUBS):
+            if x_step:
+                remote(marks_out.at[0], marks_in.at[s, ctx], marka_send, mark_recv, (dp, head * 2)).start()
+            remote(marks_out.at[1], marks_in.at[s, ctx], markb_send, mark_recv,
+                   (far[s], head * 2 + 1)).start()
 
     def send_rows(part, which_e):
         ranks = pl.ds(0, EARLY) if part == 0 else pl.ds(EARLY, PLACES - EARLY)
         for e in which_e:
-            server_y = at_y(-y_step(e, core))
             for other in range(2):
                 copy = lax.rem(core + other, 2)
-                home = lax.rem(server_y + 4 * copy, NY)
-                for x_step in (1, 3, 2, 0):
-                    head = lax.rem(x + x_step, NX)
-                    src = rows.at[head * NY + home, ranks]
-                    dst = got.at[(e % 2) * 16 + ctx * 2 + e // 2, ranks]
-                    if e == 1 and other == 0 and x_step == 0:
-                        pltpu.make_async_copy(src, dst, row_recv.at[part]).start()
-                    else:
-                        remote(src, dst, row_send.at[part], row_recv.at[part],
-                               (z * NY + server_y, head * 2 + copy)).start()
+                for s in range(SUBS):
+                    server_y = at_y(-y_step(e, copy, s))
+                    home = lax.rem(server_y + NY - away(copy, s), NY)
+                    for x_step in (1, 3, 2, 0):
+                        head = lax.rem(x + x_step, NX)
+                        src = rows.at[head * NY + home, s, ranks]
+                        dst = got.at[(e % 2) * 16 + ctx * 2 + e // 2, s, ranks]
+                        if e == 1 and other == 0 and x_step == 0:
+                            pltpu.make_async_copy(src, dst, row_recv.at[part]).start()
+                        else:
+                            remote(src, dst, row_send.at[part], row_recv.at[part],
+                                   (z * NY + server_y, head * 2 + copy)).start()
 
     def piece(chunk, i):
         return kv.at[chunk, pl.ds(lax.rem(x + STEPS[i], NX) * 2, 2)]
@@ -247,8 +267,9 @@
     col16 = lax.broadcasted_iota(jnp.int32, (16, 128), 1)
     wait_bytes(marks_in, mark_recv)
     thin = (col16 == row16 * GROUP).astype(jnp.float32).astype(jnp.bfloat16)
-    marks[z] = jnp.dot(thin, marks_in[...].reshape(128, 128),
-                       preferred_element_type=jnp.float32).astype(jnp.bfloat16)
+    found = [jnp.dot(thin, marks_in[s].reshape(128, 128), preferred_element_type=jnp.float32)
+             for s in range(SUBS)]
+    marks[z] = jnp.where(lax.rem(lax.div(col16, 32), 2) == 0, *found).astype(jnp.bfloat16)
     for dev in ring_line:
         remote(marks.at[z], marks.at[z], marks_send, marks_recv, dev).start()
     begin_on(1, (1, 2))
@@ -261,7 +282,7 @@
     lane = lax.broadcasted_iota(jnp.int32, (128, 128), 0)
     key_pos = lax.broadcasted_iota(jnp.int32, (256, SEQ), 1).astype(jnp.float32)
     lse_lane = lax.broadcasted_iota(jnp.int32, (256, 128), 1)
-    server_home = at_y(4 * core)
+    server_home = [at_y(-away(core, s)) for s in range(SUBS)]
 
     def pick(base):
         return jnp.where(lane == base, 16.0, jnp.where(lane == base + 1, 1.0, 0.0)).astype(jnp.bfloat16)
@@ -284,10 +305,10 @@
         return carry
 
     def one_sequence(n, chunk, s):
-        q = got[:, n, 0, s].reshape(256, HEAD_DIM)
-        g = got[:, n, 1, s].reshape(256, HEAD_DIM)
-        k = kv[chunk, :, pl.ds(pl.multiple_of(s * HALF, HALF), HALF), :].reshape(SEQ, HEAD_DIM)
-        v = kv[chunk, :, pl.ds(pl.multiple_of(128 + s * HALF, HALF), HALF), :].reshape(SEQ, HEAD_DIM)
+        q = got[:, s, n, 0].reshape(256, HEAD_DIM)
+        g = got[:, s, n, 1].reshape(256, HEAD_DIM)
+        k = kv[chunk, :, pl.ds(pl.multiple_of(s * 128, 128), HALF), :].reshape(SEQ, HEAD_DIM)
+        v = kv[chunk, :, pl.ds(pl.multiple_of(s * 128 + HALF, HALF), HALF), :].reshape(SEQ, HEAD_DIM)
         last, first = [jnp.concatenate([bounds[chunk * SUBS + s, which]] * 4, axis=1)
                        for which in range(2)]
         visible = jnp.logical_and(key_pos <= last, key_pos >= first)
@@ -301,8 +322,8 @@
         grad = dot(g, v, ((1,), (1,)))
         ds = (p * (grad - delta)).astype(jnp.bfloat16)
         dq = (dot(ds, k, ((1,), (0,))) * (inverse * scale)).astype(jnp.bfloat16)
-        res[:, n * 4 + s] = att.reshape(SLOTS, GROUP, HEAD_DIM)
-        res[:, n * 4 + 2 + s] = dq.reshape(SLOTS, GROUP, HEAD_DIM)
+        res[:, n * 4 + 2 * s] = att.reshape(SLOTS, GROUP, HEAD_DIM)
+        res[:, n * 4 + 2 * s + 1] = dq.reshape(SLOTS, GROUP, HEAD_DIM)
         left_over = (top + jnp.log2(total)) * math.log(2.0)
         kept = lse[...]
         for part in range(3):
@@ -311,26 +332,28 @@
             kept = jnp.where(lse_lane == part * 16 + chunk * SUBS + s, term, kept)
         lse[...] = kept
 
-    def give(tiles):
-        dst = out.at[x, server_home, tiles]
+    def give(first_tile, count):
         for e in (0, 2, 3, 1):
-            for other in range(2):
-                home_core = lax.rem(core + other, 2)
-                home_y = at_y(y_step(e, home_core))
-                for x_step in (1, 3, 2, 0):
-                    home_ctx = lax.rem(x + x_step, NX) * 2 + home_core
-                    src = res.at[(e % 2) * 16 + home_ctx * 2 + e // 2, tiles]
-                    if e == 1 and other == 0 and x_step == 0:
-                        pltpu.make_async_copy(src, dst, res_recv).start()
-                    else:
-                        remote(src, dst, res_send, res_recv, (z * NY + home_y, home_ctx)).start()
+            for s in range(SUBS):
+                tiles = pl.ds(first_tile + s * count, count)
+                dst = out.at[x, server_home[s], tiles]
+                home_y = at_y(y_step(e, core, s))
+                for other in range(2):
+                    home_core = lax.rem(core + other, 2)
+                    for x_step in (1, 3, 2, 0):
+                        home_ctx = lax.rem(x + x_step, NX) * 2 + home_core
+                        src = res.at[(e % 2) * 16 + home_ctx * 2 + e // 2, tiles]
+                        if e == 1 and other == 0 and x_step == 0:
+                            pltpu.make_async_copy(src, dst, res_recv).start()
+                        else:
+                            remote(src, dst, res_send, res_recv, (z * NY + home_y, home_ctx)).start()
 
     def rest_of_rows():
-        wait_bytes(got.at[:, pl.ds(EARLY, PLACES - EARLY)], row_recv.at[1])
+        wait_bytes(got.at[:, :, pl.ds(EARLY, PLACES - EARLY)], row_recv.at[1])
 
     def before(n):
         if n == 0:
-            wait_bytes(got.at[:, pl.ds(0, EARLY)], row_recv.at[0])
+            wait_bytes(got.at[:, :, pl.ds(0, EARLY)], row_recv.at[0])
         elif n == 1:
             pass_on(1, (0,))
         elif n == 2:
@@ -356,7 +379,7 @@
             return inner
 
         lax.fori_loop(0, SUBS, sub, 0)
-        give(pl.ds(n * 4, 4))
+        give(n * 4, 2)
         return carry
 
     lse[...] = jnp.zeros_like(lse)
@@ -364,25 +387,26 @@
     wait_bytes(marks.at[pl.ds(0, NZ - 1)], marks_recv)
     lax.fori_loop(0, NZ, make_bounds, 0)
     lax.fori_loop(0, PLACES, serve, 0)
-    res[:, 4 * PLACES] = lse[...].astype(jnp.bfloat16).reshape(SLOTS, GROUP, 128)
-    give(pl.ds(4 * PLACES, 1))
+    for s in range(SUBS):
+        res[:, 4 * PLACES + s] = lse[...].astype(jnp.bfloat16).reshape(SLOTS, GROUP, 128)
+    give(4 * PLACES, 1)
 
     sent = pl.ds(0, SLOTS - 1)
-    wait_bytes(rows.at[sent, pl.ds(0, EARLY)], row_send.at[0])
-    wait_bytes(rows.at[sent, pl.ds(EARLY, PLACES - EARLY)], row_send.at[1])
+    wait_bytes(rows.at[sent, :, pl.ds(0, EARLY)], row_send.at[0])
+    wait_bytes(rows.at[sent, :, pl.ds(EARLY, PLACES - EARLY)], row_send.at[1])
     wait_bytes(kv.at[0, pl.ds(0, 4)], kvb_send)
-    wait_bytes(marks_in.at[pl.ds(0, 4)], markb_send)
+    wait_bytes(marks_in.at[0], markb_send)
     wait_bytes(marks.at[pl.ds(0, NZ - 1)], marks_send)
 
     @pl.when(core == 0)
     def _():
         wait_bytes(kv.at[0, pl.ds(0, 3)], kva_send)
-        wait_bytes(marks_in.at[pl.ds(0, 3)], marka_send)
+        wait_bytes(marks_in.at[0, pl.ds(0, 6)], marka_send)
 
     @pl.when(core != 0)
     def _():
         wait_bytes(kv.at[0, pl.ds(0, 4)], kva_send)
-        wait_bytes(marks_in.at[pl.ds(0, 4)], marka_send)
+        wait_bytes(marks_in.at[0], marka_send)
 
     for step in range(4):
         for way in range(2):
@@ -396,7 +420,7 @@
     z = lax.div(lax.axis_index("dp"), NY)
 
     def load_part(n):
-        tiles = pl.ds(4 * n, 4) if n < PLACES else pl.ds(4 * PLACES, 1)
+        tiles = pl.ds(4 * n, 4) if n < PLACES else pl.ds(4 * PLACES, SUBS)
         return pltpu.make_async_copy(got.at[:, :, tiles], held.at[:, :, tiles], load.at[n])
 
     def store_part(n, which):
@@ -415,7 +439,9 @@
     target = jnp.where(source < 48, target, -128)
     total = jnp.zeros((HEADS, 128), jnp.float32)
     for home_y in range(NY):
-        terms = held[:, home_y, 4 * PLACES].reshape(HEADS, 128)
+        terms = [held[:, home_y, 4 * PLACES + s].reshape(HEADS, 128).astype(jnp.float32)
+                 for s in range(SUBS)]
+        terms = jnp.where(lax.rem(column[:HEADS], 2) == 0, *terms).astype(jnp.bfloat16)
         place = (column == target + home_y * SUBS).astype(jnp.float32).astype(jnp.bfloat16)
         total = total + jnp.dot(terms, place, preferred_element_type=jnp.float32)
     lse_rows[...] = total
@@ -427,7 +453,7 @@
             lines, result, copy = store_part(n, which)
             for head in range(KV_HEADS):
                 cols = slice(head * GROUP * HEAD_DIM, (head + 1) * GROUP * HEAD_DIM)
-                block = held[head, :, 4 * n + 2 * which:4 * n + 2 * which + 2]
+                block = jnp.stack([held[head, :, 4 * n + 2 * s + which] for s in range(SUBS)], axis=1)
                 result[lines, cols] = block.reshape(16, GROUP * HEAD_DIM)
             copy.start()
     for n in range(PLACES):
@@ -454,14 +480,14 @@
             pltpu.VMEM((128, thin), bf16),
             pltpu.VMEM((SUBS, 8), jnp.int32),
             pltpu.VMEM((SUBS, HALF), jnp.int32),
-            pltpu.VMEM((SLOTS, PLACES, 2, SUBS, GROUP, HEAD_DIM), bf16),
+            pltpu.VMEM((SLOTS, SUBS, PLACES, 2, GROUP, HEAD_DIM), bf16),
             pltpu.VMEM((KV_HEADS, KV_ROWS, HEAD_DIM), bf16),
             pltpu.VMEM((2, 16, 128), bf16),
-            pltpu.VMEM((NCTX, 16, 128), bf16),
+            pltpu.VMEM((SUBS, NCTX, 16, 128), bf16),
             pltpu.VMEM((NZ, 16, 128), bf16),
             pltpu.VMEM((NZ * SUBS, 2, SLOTS * GROUP, 128), jnp.float32),
             pltpu.VMEM((NZ, NCTX, KV_ROWS, HEAD_DIM), bf16),
-            pltpu.VMEM((SLOTS, PLACES, 2, SUBS, GROUP, HEAD_DIM), bf16),
+            pltpu.VMEM((SLOTS, SUBS, PLACES, 2, GROUP, HEAD_DIM), bf16),
             pltpu.VMEM((SLOTS, TILES, GROUP, HEAD_DIM), bf16),
             pltpu.VMEM((SLOTS * GROUP, 128), jnp.float32),
             pltpu.SemaphoreType.REGULAR,

time: 79.7 us -> 78.4 us (0.984)
  Pallas kernels: 78.9 us -> 77.6 us
    pallas_call x1, Pallas kernels: 76.3 us -> 74.9 us  [local(): pl.pallas_call(kernel, out_shape=jax.ShapeDtypeStruct((KV_HEADS, NY, TILE...]
where the time goes in v6:
time: 78.4 us; the launch traced here: 78.2 us
  Pallas kernels  77.6 us (99%)
    pallas_call x1, Pallas kernels, local(): pl.pallas_call(kernel, out_shape=jax.ShapeDtypeStruct((KV_HEADS, NY, TILE...  74.9 us
    pallas_call x1, Pallas kernels, local(): pl.pallas_call(order_results, out_shape=(jax.ShapeDtypeStruct((NZ * 16, w...  2.64 us

profile of v6, /device:TPU:1, one launch (start us, length us, event | category | flops | bytes accessed | tf_op | source)
XLA Modules:
  0.0 78.2 jit_solution(11885795897288373348)
XLA Ops:
  0.6 74.9 %shard_map.85.got = bf16[4,8,34,8,128]{4,3,2,1,0:T(8,128)(2,1)} custom-call(bf16[128,4096]{1,0:T(8,128)(2,1)} %queries.1, bf16[128,4096]{1,0:T(8,128)(2,1)} %grads.1, bf16[128,512]{1,0:T(8,128)(2,1)} %keys.1, bf16[128,512]{1,0:T(8,128)(2,1)} %values.1, s32[2,8]{1,0:T(2,128)} %lengths.1, s32[2,64]{1,0:T(2,128)} %bitcast.5), custom_call_target="tpu_custom_call" | custom-call | flops 4000000000 | bytes 8388608 | tf_op jit(solution)/shard_map/pallas_call | solution.py:471
  75.6 2.6 %shard_map.86 = (bf16[128,4096]{1,0:T(8,128)(2,1)}, f32[32,128]{1,0:T(8,128)}, bf16[128,4096]{1,0:T(8,128)(2,1)}) custom-call(bf16[4,8,34,8,128]{4,3,2,1,0:T(8,128)(2,1)} %shard_map.85.got), custom_call_target="tpu_custom_call" | custom-call | bytes 4194304 | tf_op jit(solution)/shard_map/pallas_call | solution.py:505

commit v7 on v6

--- a/solution.py
+++ b/solution.py
@@ -307,8 +307,8 @@
     def one_sequence(n, chunk, s):
         q = got[:, s, n, 0].reshape(256, HEAD_DIM)
         g = got[:, s, n, 1].reshape(256, HEAD_DIM)
-        k = kv[chunk, :, pl.ds(pl.multiple_of(s * 128, 128), HALF), :].reshape(SEQ, HEAD_DIM)
-        v = kv[chunk, :, pl.ds(pl.multiple_of(s * 128 + HALF, HALF), HALF), :].reshape(SEQ, HEAD_DIM)
+        k = kv[chunk, :, pl.ds(s * 128, HALF), :].reshape(SEQ, HEAD_DIM)
+        v = kv[chunk, :, pl.ds(s * 128 + HALF, HALF), :].reshape(SEQ, HEAD_DIM)
         last, first = [jnp.concatenate([bounds[chunk * SUBS + s, which]] * 4, axis=1)
                        for which in range(2)]
         visible = jnp.logical_and(key_pos <= last, key_pos >= first)
@@ -332,21 +332,20 @@
             kept = jnp.where(lse_lane == part * 16 + chunk * SUBS + s, term, kept)
         lse[...] = kept
 
-    def give(first_tile, count):
+    def give(first_tile, count, s):
+        tiles = pl.ds(first_tile + s * count, count)
+        dst = out.at[x, server_home[s], tiles]
         for e in (0, 2, 3, 1):
-            for s in range(SUBS):
-                tiles = pl.ds(first_tile + s * count, count)
-                dst = out.at[x, server_home[s], tiles]
-                home_y = at_y(y_step(e, core, s))
-                for other in range(2):
-                    home_core = lax.rem(core + other, 2)
-                    for x_step in (1, 3, 2, 0):
-                        home_ctx = lax.rem(x + x_step, NX) * 2 + home_core
-                        src = res.at[(e % 2) * 16 + home_ctx * 2 + e // 2, tiles]
-                        if e == 1 and other == 0 and x_step == 0:
-                            pltpu.make_async_copy(src, dst, res_recv).start()
-                        else:
-                            remote(src, dst, res_send, res_recv, (z * NY + home_y, home_ctx)).start()
+            home_y = at_y(y_step(e, core, s))
+            for other in range(2):
+                home_core = lax.rem(core + other, 2)
+                for x_step in (1, 3, 2, 0):
+                    home_ctx = lax.rem(x + x_step, NX) * 2 + home_core
+                    src = res.at[(e % 2) * 16 + home_ctx * 2 + e // 2, tiles]
+                    if e == 1 and other == 0 and x_step == 0:
+                        pltpu.make_async_copy(src, dst, res_recv).start()
+                    else:
+                        remote(src, dst, res_send, res_recv, (z * NY + home_y, home_ctx)).start()
 
     def rest_of_rows():
         wait_bytes(got.at[:, :, pl.ds(EARLY, PLACES - EARLY)], row_recv.at[1])
@@ -374,12 +373,9 @@
             pl.when(n == turn)(functools.partial(before, turn))
         chunk = lax.rem(z + lax.div(n + 1, 2) * (2 * lax.rem(n, 2) - 1) + NZ, NZ)
 
-        def sub(s, inner):
+        for s in range(SUBS):
             one_sequence(n, chunk, s)
-            return inner
-
-        lax.fori_loop(0, SUBS, sub, 0)
-        give(n * 4, 2)
+            give(n * 4, 2, s)
         return carry
 
     lse[...] = jnp.zeros_like(lse)
@@ -389,7 +385,8 @@
     lax.fori_loop(0, PLACES, serve, 0)
     for s in range(SUBS):
         res[:, 4 * PLACES + s] = lse[...].astype(jnp.bfloat16).reshape(SLOTS, GROUP, 128)
-    give(4 * PLACES, 1)
+    for s in range(SUBS):
+        give(4 * PLACES, 1, s)
 
     sent = pl.ds(0, SLOTS - 1)
     wait_bytes(rows.at[sent, :, pl.ds(0, EARLY)], row_send.at[0])

time: 78.4 us -> 78.3 us (level)
  no operation moved by 1% of the time
where the time goes in v7:
time: 78.3 us; the launch traced here: 78.1 us
  Pallas kernels  77.5 us (99%)
    pallas_call x1, Pallas kernels, local(): pl.pallas_call(kernel, out_shape=jax.ShapeDtypeStruct((KV_HEADS, NY, TILE...  74.8 us
    pallas_call x1, Pallas kernels, local(): pl.pallas_call(order_results, out_shape=(jax.ShapeDtypeStruct((NZ * 16, w...  2.64 us

profile of v7, /device:TPU:1, one launch (start us, length us, event | category | flops | bytes accessed | tf_op | source)
XLA Modules:
  0.0 78.1 jit_solution(15144428724193776010)
XLA Ops:
  0.6 74.8 %shard_map.85.got = bf16[4,8,34,8,128]{4,3,2,1,0:T(8,128)(2,1)} custom-call(bf16[128,4096]{1,0:T(8,128)(2,1)} %queries.1, bf16[128,4096]{1,0:T(8,128)(2,1)} %grads.1, bf16[128,512]{1,0:T(8,128)(2,1)} %keys.1, bf16[128,512]{1,0:T(8,128)(2,1)} %values.1, s32[2,8]{1,0:T(2,128)} %lengths.1, s32[2,64]{1,0:T(2,128)} %bitcast.5), custom_call_target="tpu_custom_call" | custom-call | flops 4000000000 | bytes 8388608 | tf_op jit(solution)/shard_map/pallas_call | solution.py:468
  75.5 2.6 %shard_map.86 = (bf16[128,4096]{1,0:T(8,128)(2,1)}, f32[32,128]{1,0:T(8,128)}, bf16[128,4096]{1,0:T(8,128)(2,1)}) custom-call(bf16[4,8,34,8,128]{4,3,2,1,0:T(8,128)(2,1)} %shard_map.85.got), custom_call_target="tpu_custom_call" | custom-call | bytes 4194304 | tf_op jit(solution)/shard_map/pallas_call | solution.py:502
